TPU v7x, 512 devices: a whole 4x8x8 slice. The times are simulated.
512 devices in a mesh: ctx: 64 (over y, x, core), head: 8 (over z).
Axes of the slice: x: 4, y: 8, z: 8, core: 2. Of those that a mesh axis runs over, the one named last changes fastest.
Arguments:
- inputs: bfloat16 [16384, 8192], P('ctx', 'head'), may hold values from -6 to 6
- b_proj: bfloat16 [1, 16384, 8, 128], P(None, 'ctx', 'head'), may hold values from -2 to 2
- c_proj: bfloat16 [1, 16384, 8, 128], P(None, 'ctx', 'head'), may hold values from -2 to 2
- step_sizes: float32 [1, 64, 16384], P(None, 'head', 'ctx'), may hold values from 0 to 0.18
- log_rate: float32 [1, 64], P(None, 'head'), may hold values from -7 to -2.1
- forget: float32 [1, 64, 16384], P(None, 'head', 'ctx'), may hold values from 0 to 1.6
- skip_gain: float32 [1, 64], P(None, 'head'), may hold values from 0.35 to 1.9
- norm_gain: float32 [1, 8192], P(None, 'head'), may hold values from 0.5 to 1.5
- target: bfloat16 [16384, 8192], P('ctx', 'head'), may hold values from -6 to 6
Outputs:
- grad_input: float32 [16384, 8192], P('ctx', 'head')
- grad_b: float32 [1, 16384, 8, 128], P(None, 'ctx', 'head')
- grad_c: float32 [1, 16384, 8, 128], P(None, 'ctx', 'head')
- grad_steps: float32 [1, 64, 16384], P(None, 'head', 'ctx')
All inputs are finite; a program needn't handle non-finite values.
Results may differ from a plain program's by a relative error of at most 0.00035.
Values sent between devices are 32-bit elements; how exact they have to be, the bound alone decides.
A program may use at most 128 MiB of HBM per device.

v0:
```python
import jax
import jax.numpy as jnp
from jax import lax
from jax.sharding import PartitionSpec as P

DEPTH_STACKED = 1
DIN = 8192


PRECISE = lax.Precision.HIGHEST
EPSILON = 1e-05


def from_behind(value, axis, steps):
    count = lax.axis_size(axis)
    leading, last = (max(0, -steps), min(count, count - steps))
    return lax.ppermute(value, axis, [(source, source + steps) for source in range(leading, last)])


def summary(tok_heads, b_heads, step_size, logdec):
    cum_decay = jnp.cumsum(logdec, axis=1)
    end_weight = jnp.exp(cum_decay[:, -1:] - cum_decay) * step_size
    local_state = jnp.einsum("hs,shp,shn->hpn", end_weight, tok_heads, b_heads, precision=PRECISE)
    return (local_state, jnp.exp(cum_decay[:, -1]))


def mixer_out(tok_heads, b_heads, c_heads, step_size, logdec, skip_row, state_in):
    cum_decay = jnp.cumsum(logdec, axis=1)
    line_number = jnp.arange(tok_heads.shape[0])
    causal_mask = line_number[:, None] >= line_number[None, :]
    gap_decay = cum_decay[:, :, None] - cum_decay[:, None, :]
    decay_mat = jnp.where(
        causal_mask[None], jnp.exp(jnp.where(causal_mask[None], gap_decay, 0.0)), 0.0
    )
    scores = jnp.einsum("thn,shn->hts", c_heads, b_heads, precision=PRECISE)
    weights = scores * decay_mat * step_size[:, None, :]
    near_part = jnp.einsum("hts,shp->thp", weights, tok_heads, precision=PRECISE)
    far_part = (
        jnp.einsum("thn,hpn->thp", c_heads, state_in, precision=PRECISE)
        * jnp.exp(cum_decay).T[:, :, None]
    )
    return near_part + far_part + skip_row[None, :, None] * tok_heads


def spread_heads(b_grp, head_count):
    return jnp.repeat(b_grp, head_count // b_grp.shape[1], axis=1)


def log_decay(step_row, rate_row, forget_row):
    return -step_row * jnp.exp(rate_row)[:, None] - forget_row


def entering_states(span_total, local_state):

    def relay_turn(turn, incoming):
        leaving = span_total[:, None, None] * incoming + local_state
        return from_behind(leaving, "ctx", 1)

    return lax.fori_loop(0, lax.axis_size("ctx") - 1, relay_turn, jnp.zeros_like(local_state))


def later_gradients(span_total, own_grad):

    def relay_back(turn, incoming):
        leaving = span_total[:, None, None] * incoming + own_grad
        return from_behind(leaving, "ctx", -1)

    return lax.fori_loop(0, lax.axis_size("ctx") - 1, relay_back, jnp.zeros_like(own_grad))


def forward_layer(current, b_grp, c_grp, step_row, rate_row, forget_row, skip_row, gain_row):
    head_count = step_row.shape[0]
    count_of_rows = current.shape[0]
    tok_heads = current.reshape(count_of_rows, head_count, -1)
    b_heads = spread_heads(b_grp, head_count)
    c_heads = spread_heads(c_grp, head_count)
    logdec = log_decay(step_row, rate_row, forget_row)
    local_state, span_total = summary(tok_heads, b_heads, step_row, logdec)
    state_in = entering_states(span_total, local_state)
    mixed = mixer_out(tok_heads, b_heads, c_heads, step_row, logdec, skip_row, state_in).reshape(
        count_of_rows, -1
    )
    squares = lax.psum(jnp.sum(mixed * mixed, axis=1), "head")
    inv_scale = lax.rsqrt(squares / DIN + EPSILON)
    updated = current + gain_row * mixed * inv_scale[:, None]
    return (updated, state_in, mixed, inv_scale)


def backward_layer(
    grad_out,
    current,
    b_grp,
    c_grp,
    step_row,
    rate_row,
    forget_row,
    skip_row,
    gain_row,
    state_in,
    mixed,
    inv_scale,
):
    head_count = step_row.shape[0]
    count_of_rows = current.shape[0]
    grad_normed = gain_row * grad_out
    inner_sum = lax.psum(jnp.sum(grad_normed * mixed, axis=1), "head")
    grad_mixed = (
        grad_normed * inv_scale[:, None] - mixed * (inner_sum * inv_scale**3 / DIN)[:, None]
    )
    grad_heads = grad_mixed.reshape(count_of_rows, head_count, -1)
    logdec = log_decay(step_row, rate_row, forget_row)
    c_heads = spread_heads(c_grp, head_count)

    def local_part(layer_in, b_local, c_local, step_local):
        piece_slice = layer_in.reshape(count_of_rows, head_count, -1)
        b_local_heads = spread_heads(b_local, head_count)
        c_local_heads = spread_heads(c_local, head_count)
        dec_local = log_decay(step_local, rate_row, forget_row)
        mixed_local = mixer_out(
            piece_slice, b_local_heads, c_local_heads, step_local, dec_local, skip_row, state_in
        )
        local_state, span_total = summary(piece_slice, b_local_heads, step_local, dec_local)
        return (mixed_local, local_state, span_total)

    (_, local_state, span_total), pullback = jax.vjp(local_part, current, b_grp, c_grp, step_row)
    cum_decay = jnp.cumsum(logdec, axis=1)
    own_grad = jnp.einsum(
        "ht,thp,thn->hpn", jnp.exp(cum_decay), grad_heads, c_heads, precision=PRECISE
    )
    grad_later = later_gradients(span_total, own_grad)
    grad_total = jnp.sum(grad_later * state_in, axis=(1, 2))
    grad_in, grad_bgrp, grad_cgrp, grad_step = pullback((grad_heads, grad_later, grad_total))
    return (grad_out + grad_in, grad_bgrp, grad_cgrp, grad_step)


def body(inputs, b_proj, c_proj, step_sizes, log_rate, forget, skip_gain, norm_gain, target):
    current = inputs.astype(jnp.float32)
    layer_idx = 0
    b_grp = b_proj[layer_idx].astype(jnp.float32)
    c_grp = c_proj[layer_idx].astype(jnp.float32)
    updated, state_in, mixed, inv_scale = forward_layer(
        current,
        b_grp,
        c_grp,
        step_sizes[layer_idx],
        log_rate[layer_idx],
        forget[layer_idx],
        skip_gain[layer_idx],
        norm_gain[layer_idx],
    )
    stored = [(current, b_grp, c_grp, state_in, mixed, inv_scale)]
    grad_out = updated - target.astype(jnp.float32)
    grads_b = []
    grads_c = []
    grads_step = []
    for layer_idx in reversed(range(DEPTH_STACKED)):
        layer_in, b_grp, c_grp, state_in, mixed, inv_scale = stored[layer_idx]
        grad_out, grad_bgrp, grad_cgrp, grad_step = backward_layer(
            grad_out,
            layer_in,
            b_grp,
            c_grp,
            step_sizes[layer_idx],
            log_rate[layer_idx],
            forget[layer_idx],
            skip_gain[layer_idx],
            norm_gain[layer_idx],
            state_in,
            mixed,
            inv_scale,
        )
        grads_b.insert(0, grad_bgrp)
        grads_c.insert(0, grad_cgrp)
        grads_step.insert(0, grad_step)
    return (grad_out, jnp.stack(grads_b), jnp.stack(grads_c), jnp.stack(grads_step))


def solution(mesh):
    in_specs = (
        P("ctx", "head"),
        P(None, "ctx", "head", None),
        P(None, "ctx", "head", None),
        P(None, "head", "ctx"),
        P(None, "head"),
        P(None, "head", "ctx"),
        P(None, "head"),
        P(None, "head"),
        P("ctx", "head"),
    )
    out_specs = (
        P("ctx", "head"),
        P(None, "ctx", "head", None),
        P(None, "ctx", "head", None),
        P(None, "head", "ctx"),
    )
    return jax.shard_map(body, mesh=mesh, in_specs=in_specs, out_specs=out_specs, check_vma=False)
```

profile of v0, /device:TPU:95, one launch (start us, length us, event | category | flops | bytes accessed | tf_op | source)
XLA Modules:
  0.0 1842.5 jit_solution(6967042432334319595)
XLA Ops:
  7.0 875.4 %while.20 = (s32[]{:T(128)}, f32[8,128,128]{2,1,0:T(8,128)S(1)}, f32[8]{0:T(128)S(1)}, f32[8,128,128]{2,1,0:T(8,128)S(1)}, s32[]{:T(128)}) while((s32[]{:T(128)}, f32[8,128,128]{2,1,0:T(8,128)S(1)}, f32[8]{0:T(128)S(1)}, f32[8,128,128]{2,1,0:T(8,128)S(1)}, s32[]{:T(128)}) %tuple.49), condition=%wide.region_3.4_spmd, body=%wide.region_2.3_spmd.sunk | while | flops 262146 | bytes 3670149 | solution.py:59
  890.0 16.4 psum.14
  906.9 13.2 psum.15
  924.2 886.4 %while.21 = (s32[]{:T(128)}, f32[8,128,128]{2,1,0:T(8,128)S(1)}, f32[8]{0:T(128)S(1)}, f32[8,128,128]{2,1,0:T(8,128)S(1)}, s32[]{:T(128)}) while((s32[]{:T(128)}, f32[8,128,128]{2,1,0:T(8,128)S(1)}, f32[8]{0:T(128)S(1)}, f32[8,128,128]{2,1,0:T(8,128)S(1)}, s32[]{:T(128)}) %tuple.55), condition=%wide.region_9.10_spmd, body=%wide.region_8.9_spmd.sunk | while | flops 262146 | bytes 3670149 | solution.py:68
  926.3 20.0 %collective-permute-done.1 = f32[8,128,128]{2,1,0:T(8,128)S(1)} collective-permute-done((f32[8,128,128]{2,1,0:T(8,128)S(1)}, f32[8,128,128]{2,1,0:T(8,128)S(1)}, u32[]{:S(2)}, u32[]{:S(2)}) %collective-permute-start.1) | collective-permute-done | bytes 524320 | tf_op jit(solution)/shard_map/while/body/eval_jaxpr/ppermute | solution.py:17
  948.3 11.9 collective-permute-done.1
  962.3 11.9 collective-permute-done.1
  976.2 11.9 collective-permute-done.1
  990.2 11.9 collective-permute-done.1
  1004.1 11.9 collective-permute-done.1
  1018.0 11.9 collective-permute-done.1
  1032.0 11.9 collective-permute-done.1
  1045.9 11.9 collective-permute-done.1
  1059.9 11.9 collective-permute-done.1
  1073.8 11.9 collective-permute-done.1
  1087.7 11.9 collective-permute-done.1
  1101.7 11.9 collective-permute-done.1
  1115.6 11.9 collective-permute-done.1
  1129.6 11.9 collective-permute-done.1
  1143.5 11.9 collective-permute-done.1
  1157.4 11.9 collective-permute-done.1
  1171.4 11.9 collective-permute-done.1
  1185.3 11.9 collective-permute-done.1
  1199.3 11.9 collective-permute-done.1
  1213.2 11.9 collective-permute-done.1
  1227.1 11.9 collective-permute-done.1
  1241.1 11.9 collective-permute-done.1
  1255.0 11.9 collective-permute-done.1
  1269.0 11.9 collective-permute-done.1
  1282.9 11.9 collective-permute-done.1
  1296.8 11.9 collective-permute-done.1
  1310.8 11.9 collective-permute-done.1
  1324.7 11.9 collective-permute-done.1
  1338.7 11.9 collective-permute-done.1
  1352.6 11.9 collective-permute-done.1
  1366.6 11.9 collective-permute-done.1
  1380.5 11.9 collective-permute-done.1
  1394.4 11.9 collective-permute-done.1
  1408.4 11.9 collective-permute-done.1
  1422.3 11.9 collective-permute-done.1
  1436.3 11.9 collective-permute-done.1
  1450.2 11.9 collective-permute-done.1
  1464.1 11.9 collective-permute-done.1
  1478.1 11.9 collective-permute-done.1
  1492.0 11.9 collective-permute-done.1
  1506.0 11.9 collective-permute-done.1
  1519.9 11.9 collective-permute-done.1
  1533.8 11.9 collective-permute-done.1
  1547.8 11.9 collective-permute-done.1
  1561.7 11.9 collective-permute-done.1
  1575.7 11.9 collective-permute-done.1
  1589.6 11.9 collective-permute-done.1
  1603.5 11.9 collective-permute-done.1
  1617.5 11.9 collective-permute-done.1
  1631.4 11.9 collective-permute-done.1
  1645.4 11.9 collective-permute-done.1
  1659.3 11.9 collective-permute-done.1
  1673.2 11.9 collective-permute-done.1
  1687.2 11.9 collective-permute-done.1
  1715.1 11.9 collective-permute-done.1
  1729.0 11.9 collective-permute-done.1
  1756.9 11.9 collective-permute-done.1
  1770.8 11.9 collective-permute-done.1
  1798.7 11.9 collective-permute-done.1
  (407 shorter events, 1088.6 us)
Async XLA Ops:
  18.3 13.8 collective-permute-start
  32.2 13.8 collective-permute-start
  46.1 13.8 collective-permute-start
  60.1 13.8 collective-permute-start
  74.0 13.8 collective-permute-start
  88.0 13.8 collective-permute-start
  101.9 13.8 collective-permute-start
  115.8 13.8 collective-permute-start
  129.8 13.8 collective-permute-start
  143.7 13.8 collective-permute-start
  157.7 13.8 collective-permute-start
  171.6 13.8 collective-permute-start
  185.5 13.8 collective-permute-start
  199.5 13.8 collective-permute-start
  213.4 13.8 collective-permute-start
  227.4 13.8 collective-permute-start
  241.3 13.8 collective-permute-start
  255.2 13.8 collective-permute-start
  269.2 13.8 collective-permute-start
  283.1 13.8 collective-permute-start
  297.1 13.8 collective-permute-start
  311.0 13.8 collective-permute-start
  324.9 13.8 collective-permute-start
  338.9 13.8 collective-permute-start
  352.8 13.8 collective-permute-start
  366.8 13.8 collective-permute-start
  380.7 13.8 collective-permute-start
  394.6 13.8 collective-permute-start
  408.6 13.8 collective-permute-start
  422.5 13.8 collective-permute-start
  436.5 13.8 collective-permute-start
  450.4 13.8 collective-permute-start
  464.4 13.8 collective-permute-start
  478.3 13.8 collective-permute-start
  492.2 13.8 collective-permute-start
  506.2 13.8 collective-permute-start
  520.1 13.8 collective-permute-start
  534.1 13.8 collective-permute-start
  548.0 13.8 collective-permute-start
  561.9 13.8 collective-permute-start
  575.9 13.8 collective-permute-start
  589.8 13.8 collective-permute-start
  603.8 13.8 collective-permute-start
  617.7 13.8 collective-permute-start
  631.6 13.8 collective-permute-start
  645.6 13.8 collective-permute-start
  659.5 13.8 collective-permute-start
  673.5 13.8 collective-permute-start
  687.4 13.8 collective-permute-start
  701.3 13.8 collective-permute-start
  715.3 13.8 collective-permute-start
  729.2 13.8 collective-permute-start
  743.2 13.8 collective-permute-start
  757.1 13.8 collective-permute-start
  771.0 13.8 collective-permute-start
  785.0 13.8 collective-permute-start
  798.9 13.8 collective-permute-start
  812.9 13.8 collective-permute-start
  826.8 13.8 collective-permute-start
  840.7 13.8 collective-permute-start
  854.7 13.8 collective-permute-start
  868.6 13.8 collective-permute-start
  924.3 21.9 %collective-permute-start.1 = (f32[8,128,128]{2,1,0:T(8,128)S(1)}, f32[8,128,128]{2,1,0:T(8,128)S(1)}, u32[]{:S(2)}, u32[]{:S(2)}) collective-permute-start(f32[8,128,128]{2,1,0:T(8,128)S(1)} %multiply_add_fusion.5), channel_id=1, source_target_pairs={{8,0},{16,8},{24,16},{32,24},{40,32},{48,40},{56,48},{64,56},{72,6... | collective-permute-start | bytes 1572872 | tf_op jit(solution)/shard_map/while/body/eval_jaxpr/ppermute | solution.py:17
  946.4 13.8 collective-permute-start.1
  (80 other events, 1862.1 us)
where the time goes:
time: 1850 us; the launch traced here: 1840 us
  waiting for transfers between devices  1140 us (62%)
  starting transfers between devices  604 us (33%)
  blocking collectives  29.6 us (2%)
  other arithmetic  27.3 us (1%)
  matrix products  25.5 us (1%)
    ppermute x126, waiting for transfers between devices, from_behind(): lax.ppermute(value, axis, [(source, source + steps) for source in range(l...  1140 us
    ppermute x126, starting transfers between devices, from_behind(): lax.ppermute(value, axis, [(source, source + steps) for source in range(l...  604 us
  transfers between devices with their start and end apart: 126, of which 126 were waited for; matrix products, arithmetic and copies ran while one was open for 0% of the time, Pallas kernels for 0%

commit v1 on v0

v1 whole, which is shorter than its diff:
```python
import functools

import jax
import jax.numpy as jnp
from jax import lax
from jax.experimental import pallas as pl
from jax.experimental.pallas import tpu as pltpu
from jax.sharding import PartitionSpec as P

EPSILON = 1e-05
MESH = pl.DeviceIdType.MESH
F32 = jnp.float32
BF16 = jnp.bfloat16
NN = (((1,), (0,)), ((), ()))
NT = (((1,), (1,)), ((), ()))

CUM, EXPCUM, ENDW, ENDDEC, STEP = range(5)


def mm(left, right, dims=NN):
    return lax.dot_general(left, right, dims, preferred_element_type=F32)


def split2(value):
    high = value.astype(BF16)
    low = (value - high.astype(F32)).astype(BF16)
    return high, low


def split3(value):
    high = value.astype(BF16)
    rest = value - high.astype(F32)
    mid = rest.astype(BF16)
    low = (rest - mid.astype(F32)).astype(BF16)
    return high, mid, low


def mm3(left, right, dims=NN):
    (lh, ll), (rh, rl) = left, right
    return mm(lh, rh, dims) + (mm(lh, rl, dims) + mm(ll, rh, dims))


def kernel(
    chips,
    ranks,
    width,
    x_ref,
    target_ref,
    b_ref,
    c_ref,
    step_ref,
    forget_ref,
    rate_ref,
    skip_ref,
    gain_ref,
    gx_ref,
    gb_ref,
    gc_ref,
    gs_ref,
    rows_ref,
    cols_ref,
    scores_ref,
    mixed_ref,
    gm_ref,
    y_ref,
    rq_ref,
    ext_ref,
    sin_ref,
    gout_ref,
    btr_ref,
    ctr_ref,
    dst_ref,
    sum_ref,
    fl_own,
    fl_got,
    fm_out,
    fm_in,
    fp_out,
    fp_in,
    fs_out,
    fs_in,
    bl_own,
    bl_got,
    bm_out,
    bm_in,
    bp_out,
    bp_in,
    bs_out,
    bs_in,
    z_out,
    z_in,
    pair_send,
    pair_recv,
    ring_send,
    ring_recv,
    z_send,
    z_recv,
):
    tokens = x_ref.shape[0]
    heads = step_ref.shape[0]
    half = heads // 2
    chan = x_ref.shape[1] // heads
    piece = half * 128 // chips
    per_head = chips // half
    ctx = lax.axis_index("ctx")
    rank = lax.axis_index("head")
    chip, core = lax.div(ctx, 2), lax.rem(ctx, 2)
    sibling = (chip * 2 + 1 - core, rank)

    def partner(turn):
        if chips != 32:
            return lax.rem(chip + 1 + turn, chips)
        row, column = lax.div(chip, 4), lax.rem(chip, 4)
        q, r = lax.div(turn, 4), lax.rem(turn, 4)
        down = 4 + (1 - 2 * lax.rem(q, 2)) * lax.div(q + 1, 2)
        along = 2 + (1 - 2 * lax.rem(r, 2)) * lax.div(r + 1, 2)
        return lax.rem(row + down, 8) * 4 + lax.rem(column + along, 4)

    def device(at_chip):
        return (at_chip * 2 + core, rank)

    def loop(low, high, step):
        def turn(i, carry):
            step(i)
            return carry

        lax.fori_loop(low, high, turn, 0)

    barrier = pltpu.get_barrier_semaphore()

    def greet(turn):
        pl.semaphore_signal(barrier, inc=1, device_id=device(partner(turn)), device_id_type=MESH)

    def greet_rank(turn):
        other = lax.rem(rank + 1 + turn, ranks)
        pl.semaphore_signal(barrier, inc=1, device_id=(ctx, other), device_id_type=MESH)

    loop(0, chips - 1, greet)
    loop(0, ranks - 1, greet_rank)
    pl.semaphore_signal(barrier, inc=1, device_id=sibling, device_id_type=MESH)

    head_iota = lax.broadcasted_iota(jnp.int32, (heads, tokens), 0)
    rate = jnp.zeros((heads, tokens), F32)
    for h in range(heads):
        rate = jnp.where(head_iota == h, rate_ref[0, h], rate)
    rate = jnp.exp(rate)
    step = step_ref[...]
    logdec = -step * rate - forget_ref[...]
    down_iota = lax.broadcasted_iota(jnp.int32, (tokens, tokens), 0)
    along_iota = lax.broadcasted_iota(jnp.int32, (tokens, tokens), 1)
    upper = (down_iota <= along_iota).astype(F32).astype(BF16)
    parts = split3(logdec)
    cum = mm(parts[0], upper) + (mm(parts[1], upper) + mm(parts[2], upper))
    last = cum[:, tokens - 1 : tokens]
    expcum = jnp.exp(cum)
    enddec = jnp.exp(last - cum)
    rows = [cum, expcum, enddec * step, enddec, step]
    for i, row in enumerate(rows):
        rows_ref[i] = row
    table = jnp.concatenate(rows + [jnp.zeros((128 - heads * len(rows), tokens), F32)], axis=0)
    cols_ref[...] = table.T
    btr_ref[...] = b_ref[...].astype(F32).T.astype(BF16)
    ctr_ref[...] = c_ref[...].astype(F32).T.astype(BF16)

    def columns_of(h):
        rolled = pltpu.roll(cols_ref[...], lax.rem(128 - h, 128), 1)
        return [rolled[:, 8 * q : 8 * q + 1] for q in range(5)]

    def channels(h):
        return pl.ds(pl.multiple_of(h * chan, chan), chan)

    def row_of(q, h):
        return rows_ref[q, pl.ds(h, 1), :]

    def decay_of(h):
        return jnp.broadcast_to(row_of(EXPCUM, h)[:, tokens - 1 : tokens], (1, 128))

    def local_state(i, h):
        weighted = x_ref[:, channels(h)].astype(F32) * columns_of(h)[ENDW]
        high, low = split2(weighted)
        fl_own[h, 0:128, :] = mm(btr_ref[...], high) + mm(btr_ref[...], low)
        fl_own[h, 128:136, :] = jnp.broadcast_to(decay_of(h), (8, 128))

    def to_sibling(source, target, sem):
        return pltpu.make_async_remote_copy(
            src_ref=source,
            dst_ref=target,
            send_sem=pair_send.at[sem],
            recv_sem=pair_recv.at[sem],
            device_id=sibling,
            device_id_type=MESH,
        )

    mine, theirs = core * half, (1 - core) * half
    loop(0, half, lambda i: local_state(i, theirs + i))
    pl.semaphore_wait(barrier, (chips - 1) + (ranks - 1) + 1)
    swap = to_sibling(fl_own.at[pl.ds(theirs, half)], fl_got, 0)
    swap.start()
    loop(0, half, lambda i: local_state(i, mine + i))
    swap.wait_recv()

    def ring_copy(source, target, rows_sent, sem, to, slot):
        return pltpu.make_async_remote_copy(
            src_ref=source.at[to, 0:rows_sent],
            dst_ref=target.at[slot, 0:rows_sent],
            send_sem=ring_send.at[sem, to],
            recv_sem=ring_recv.at[sem, slot],
            device_id=device(to),
            device_id_type=MESH,
        )

    def ring_start(source, target, rows_sent, sem):
        def start(turn):
            ring_copy(source, target, rows_sent, sem, partner(turn), chip).start()

        loop(0, chips - 1, start)
        target[chip, 0:rows_sent, :] = source[chip, 0:rows_sent, :]

    def ring_arrived(source, target, rows_sent, sem):
        def arrived(turn):
            other = partner(turn)
            ring_copy(source, target, rows_sent, sem, other, other).wait_recv()

        loop(0, chips - 1, arrived)

    def ring_sent(source, target, rows_sent, sem):
        def sent(turn):
            other = partner(turn)
            ring_copy(source, target, rows_sent, sem, other, other).wait_send()

        loop(0, chips - 1, sent)

    def pair_of(own, got, i):
        own_rows, got_rows = own[mine + i, 0:128, :], got[i, 0:128, :]
        first = jnp.where(core == 0, own_rows, got_rows)
        second = jnp.where(core == 0, got_rows, own_rows)
        return first, second

    def decay_pair(i):
        own_decay, got_decay = fl_own[mine + i, 128:129, :], fl_got[i, 128:129, :]
        first = jnp.where(core == 0, own_decay, got_decay)
        second = jnp.where(core == 0, got_decay, own_decay)
        return first, second

    def join_forward(i):
        first, second = pair_of(fl_own, fl_got, i)
        decay0, decay1 = decay_pair(i)
        joined = decay1 * first + second
        decay = jnp.broadcast_to(decay0 * decay1, (8, 128))
        for j in range(per_head):
            fm_out[i * per_head + j, 0:piece, :] = joined[j * piece : (j + 1) * piece, :]
            fm_out[i * per_head + j, piece : piece + 8, :] = decay

    loop(0, half, join_forward)
    ring_start(fm_out, fm_in, piece + 1, 0)

    scores_ref[...] = mm(c_ref[...], b_ref[...], NT)

    def near(h):
        cols = columns_of(h)
        gap = jnp.where(down_iota >= along_iota, cols[CUM] - row_of(CUM, h), -1e30)
        weights = scores_ref[...] * jnp.exp(gap) * row_of(STEP, h)
        high, low = split2(weights)
        x_h = x_ref[:, channels(h)]
        mixed_ref[:, channels(h)] = mm(high, x_h) + mm(low, x_h)

    loop(0, heads, near)

    ring_arrived(fm_out, fm_in, piece + 1, 0)

    def scan_forward(t, state):
        fp_out[t] = state
        return fm_in[t, piece : piece + 1, :] * state + fm_in[t, 0:piece, :]

    lax.fori_loop(0, chips, scan_forward, jnp.zeros((piece, 128), F32))
    ring_start(fp_out, fp_in, piece, 1)
    ring_arrived(fp_out, fp_in, piece, 1)

    def enter(i):
        first, _ = pair_of(fl_own, fl_got, i)
        decay0, _ = decay_pair(i)
        for_first = jnp.concatenate([fp_in[i * per_head + j] for j in range(per_head)], axis=0)
        for_second = decay0 * for_first + first
        sin_ref[mine + i] = jnp.where(core == 0, for_first, for_second)
        fs_out[i] = jnp.where(core == 0, for_second, for_first)

    loop(0, half, enter)
    swap_in = to_sibling(fs_out, fs_in, 1)
    swap_in.start()

    sum_ref[...] = jnp.zeros_like(sum_ref)

    def far(h):
        cols = columns_of(h)
        high, low = split2(sin_ref[h])
        reached = mm(c_ref[...], high) + mm(c_ref[...], low)
        x_h = x_ref[:, channels(h)].astype(F32)
        mixed = mixed_ref[:, channels(h)] + cols[EXPCUM] * reached + skip_ref[0, h] * x_h
        mixed_ref[:, channels(h)] = mixed
        gained = gain_ref[:, channels(h)] * mixed
        sum_ref[0] += mixed * mixed
        sum_ref[1] += gained * (x_h - target_ref[:, channels(h)].astype(F32))
        sum_ref[2] += gained * gained

    loop(0, half, lambda i: far(mine + i))
    swap_in.wait_recv()

    def take(i):
        sin_ref[theirs + i] = fs_in[i]

    loop(0, half, take)
    loop(0, half, lambda i: far(theirs + i))

    lane = lax.broadcasted_iota(jnp.int32, (tokens, 128), 1)
    packed = jnp.zeros((tokens, 128), F32)
    for i in range(3):
        packed = jnp.where(lane == i, jnp.sum(sum_ref[i], axis=1, keepdims=True), packed)
    z_out[...] = packed.T[0:8, :]

    def z_copy(to, slot):
        return pltpu.make_async_remote_copy(
            src_ref=z_out,
            dst_ref=z_in.at[slot],
            send_sem=z_send.at[to],
            recv_sem=z_recv.at[slot],
            device_id=(ctx, to),
            device_id_type=MESH,
        )

    def z_start(turn):
        z_copy(lax.rem(rank + 1 + turn, ranks), rank).start()

    def z_arrived(turn):
        other = lax.rem(rank + 1 + turn, ranks)
        z_copy(other, other).wait_recv()

    def z_sent(turn):
        other = lax.rem(rank + 1 + turn, ranks)
        z_copy(other, other).wait_send()

    loop(0, ranks - 1, z_start)
    z_in[rank] = z_out[...]
    loop(0, ranks - 1, z_arrived)
    total = z_in[0]
    for i in range(1, ranks):
        total = total + z_in[i]
    inv_scale = lax.rsqrt(total[0:1, :] / width + EPSILON)
    inner = total[1:2, :] + inv_scale * total[2:3, :]
    coef = inner * inv_scale * inv_scale * inv_scale / width
    back = jnp.concatenate([inv_scale, coef, jnp.zeros((126, tokens), F32)], axis=0).T
    inv_col, coef_col = back[:, 0:1], back[:, 1:2]

    def norm_back(h):
        gain = gain_ref[:, channels(h)]
        mixed = mixed_ref[:, channels(h)]
        x_h = x_ref[:, channels(h)].astype(F32)
        grad_out = x_h + gain * mixed * inv_col - target_ref[:, channels(h)].astype(F32)
        grad_mixed = gain * grad_out * inv_col - mixed * coef_col
        gm_ref[:, channels(h)] = grad_mixed
        gx_ref[:, channels(h)] = grad_out + skip_ref[0, h] * grad_mixed
        high, low = split2(grad_mixed * columns_of(h)[EXPCUM])
        bl_own[h] = mm(ctr_ref[...], high) + mm(ctr_ref[...], low)

    loop(0, half, lambda i: norm_back(theirs + i))
    swap_back = to_sibling(bl_own.at[pl.ds(theirs, half)], bl_got, 2)
    swap_back.start()
    loop(0, half, lambda i: norm_back(mine + i))
    swap_back.wait_recv()

    def join_back(i):
        first, second = pair_of(bl_own, bl_got, i)
        decay0, _ = decay_pair(i)
        joined = decay0 * second + first
        for j in range(per_head):
            bm_out[i * per_head + j] = joined[j * piece : (j + 1) * piece, :]

    loop(0, half, join_back)
    ring_start(bm_out, bm_in, piece, 2)

    rq_ref[...] = jnp.zeros_like(rq_ref)
    gc_ref[...] = jnp.zeros_like(gc_ref)
    gb_ref[...] = jnp.zeros_like(gb_ref)
    dst_ref[...] = jnp.zeros_like(dst_ref)
    scores_ref[...] = mm(b_ref[...], c_ref[...], NT)

    def near_back(h):
        cols = columns_of(h)
        gap = jnp.where(along_iota >= down_iota, row_of(CUM, h) - cols[CUM], -1e30)
        decay = jnp.exp(gap)
        grad_mixed = gm_ref[:, channels(h)]
        gm_parts = split2(grad_mixed)
        x_h = x_ref[:, channels(h)]
        y_ref[:, channels(h)] = mm3(split2(scores_ref[...] * decay), gm_parts)
        grad_weights = mm(x_h, gm_parts[0], NT) + mm(x_h, gm_parts[1], NT)
        dst_ref[...] += grad_weights * decay * cols[STEP]
        own = grad_mixed * (mixed_ref[:, channels(h)] - skip_ref[0, h] * x_h.astype(F32))
        rq_ref[...] = jnp.where(lane == h, jnp.sum(own, axis=1, keepdims=True), rq_ref[...])
        gc_ref[...] += mm3(split2(grad_mixed * cols[EXPCUM]), split2(sin_ref[h]), NT)

    loop(0, heads, near_back)
    grad_scores = dst_ref[...]
    high, low = split2(grad_scores)
    gb_ref[...] += mm(high, c_ref[...]) + mm(low, c_ref[...])
    high, low = split2(grad_scores.T)
    gc_ref[...] += mm(high, b_ref[...]) + mm(low, b_ref[...])

    ring_arrived(bm_out, bm_in, piece, 2)

    def scan_back(turn, grad):
        t = chips - 1 - turn
        bp_out[t] = grad
        return fm_in[t, piece : piece + 1, :] * grad + bm_in[t]

    lax.fori_loop(0, chips, scan_back, jnp.zeros((piece, 128), F32))
    ring_start(bp_out, bp_in, piece, 3)
    ring_arrived(bp_out, bp_in, piece, 3)

    def leave(i):
        _, second = pair_of(bl_own, bl_got, i)
        _, decay1 = decay_pair(i)
        for_second = jnp.concatenate([bp_in[i * per_head + j] for j in range(per_head)], axis=0)
        for_first = decay1 * for_second + second
        gout_ref[mine + i] = jnp.where(core == 0, for_first, for_second)
        bs_out[i] = jnp.where(core == 0, for_second, for_first)

    loop(0, half, leave)
    swap_out = to_sibling(bs_out, bs_in, 3)
    swap_out.start()

    def far_back(h):
        cols = columns_of(h)
        grad_state = gout_ref[h]
        high, low = split2(grad_state)
        x_h = x_ref[:, channels(h)]
        reached = mm(b_ref[...], high) + mm(b_ref[...], low)
        value = y_ref[:, channels(h)] + cols[ENDDEC] * reached
        gx_ref[:, channels(h)] += cols[STEP] * value
        own = jnp.sum(x_h.astype(F32) * value, axis=1, keepdims=True)
        rq_ref[...] = jnp.where(lane == h + 8, own, rq_ref[...])
        gb_ref[...] += cols[ENDW] * (mm(x_h, high, NT) + mm(x_h, low, NT))
        leaving = decay_of(h) * sin_ref[h] + fl_own[h, 0:128, :]
        ext_ref[pl.ds(h, 1), :] = jnp.sum(grad_state * leaving, axis=0, keepdims=True)

    loop(0, half, lambda i: far_back(mine + i))
    swap_out.wait_recv()

    def take_back(i):
        gout_ref[theirs + i] = bs_in[i]

    loop(0, half, take_back)
    loop(0, half, lambda i: far_back(theirs + i))

    ends = rq_ref[...].T
    inner_x = ends[8 : 8 + heads, :]
    extra = jnp.sum(ext_ref[...], axis=1, keepdims=True)
    token_iota = lax.broadcasted_iota(jnp.int32, (heads, tokens), 1)
    grad_cum = ends[0:heads, :] - step * inner_x + jnp.where(token_iota == tokens - 1, extra, 0.0)
    lower = (down_iota >= along_iota).astype(F32).astype(BF16)
    parts = split3(grad_cum)
    grad_dec = mm(parts[0], lower) + (mm(parts[1], lower) + mm(parts[2], lower))
    gs_ref[...] = inner_x - rate * grad_dec

    swap.wait_send()
    swap_in.wait_send()
    swap_back.wait_send()
    swap_out.wait_send()
    ring_sent(fm_out, fm_in, piece + 1, 0)
    ring_sent(fp_out, fp_in, piece, 1)
    ring_sent(bm_out, bm_in, piece, 2)
    ring_sent(bp_out, bp_in, piece, 3)
    loop(0, ranks - 1, z_sent)


def body(chips, ranks, inputs, b_proj, c_proj, step_sizes, log_rate, forget, skip_gain, norm_gain, target):
    tokens, wide = inputs.shape
    heads = step_sizes.shape[1]
    half = heads // 2
    piece = half * 128 // chips
    vmem = pl.BlockSpec(memory_space=pltpu.VMEM)
    smem = pl.BlockSpec(memory_space=pltpu.SMEM)

    def buffer(*shape, dtype=F32):
        return pltpu.VMEM(shape, dtype)

    state = (heads, 128, 128)
    half_state = (half, 128, 128)
    grad_x, grad_b, grad_c, grad_steps = pl.pallas_call(
        functools.partial(kernel, chips, ranks, float(wide * ranks)),
        out_shape=(
            jax.ShapeDtypeStruct((tokens, wide), F32),
            jax.ShapeDtypeStruct((tokens, 128), F32),
            jax.ShapeDtypeStruct((tokens, 128), F32),
            jax.ShapeDtypeStruct((heads, tokens), F32),
        ),
        in_specs=[vmem] * 6 + [smem] * 2 + [vmem],
        out_specs=[vmem] * 4,
        scratch_shapes=[
            buffer(5, heads, tokens),
            buffer(tokens, 128),
            buffer(tokens, tokens),
            buffer(tokens, wide),
            buffer(tokens, wide),
            buffer(tokens, wide),
            buffer(tokens, 128),
            buffer(heads, 128),
            buffer(*state),
            buffer(*state),
            buffer(128, tokens, dtype=BF16),
            buffer(128, tokens, dtype=BF16),
            buffer(tokens, tokens),
            buffer(3, tokens, 128),
            buffer(heads, 136, 128),
            buffer(half, 136, 128),
            buffer(chips, piece + 8, 128),
            buffer(chips, piece + 8, 128),
            buffer(chips, piece, 128),
            buffer(chips, piece, 128),
            buffer(*half_state),
            buffer(*half_state),
            buffer(*state),
            buffer(*half_state),
            buffer(chips, piece, 128),
            buffer(chips, piece, 128),
            buffer(chips, piece, 128),
            buffer(chips, piece, 128),
            buffer(*half_state),
            buffer(*half_state),
            buffer(8, tokens),
            buffer(ranks, 8, tokens),
            pltpu.SemaphoreType.DMA((4,)),
            pltpu.SemaphoreType.DMA((4,)),
            pltpu.SemaphoreType.DMA((4, chips)),
            pltpu.SemaphoreType.DMA((4, chips)),
            pltpu.SemaphoreType.DMA((ranks,)),
            pltpu.SemaphoreType.DMA((ranks,)),
        ],
        compiler_params=pltpu.CompilerParams(
            collective_id=0, has_side_effects=True, vmem_limit_bytes=40 * 1024 * 1024
        ),
        name="layer",
    )(
        inputs,
        target,
        b_proj.reshape(tokens, 128),
        c_proj.reshape(tokens, 128),
        step_sizes[0],
        forget[0],
        log_rate,
        skip_gain,
        norm_gain,
    )
    return (
        grad_x,
        grad_b.reshape(1, tokens, 1, 128),
        grad_c.reshape(1, tokens, 1, 128),
        grad_steps[None],
    )


def solution(mesh):
    chips, ranks = mesh.shape["ctx"] // 2, mesh.shape["head"]
    in_specs = (
        P("ctx", "head"),
        P(None, "ctx", "head", None),
        P(None, "ctx", "head", None),
        P(None, "head", "ctx"),
        P(None, "head"),
        P(None, "head", "ctx"),
        P(None, "head"),
        P(None, "head"),
        P("ctx", "head"),
    )
    out_specs = (
        P("ctx", "head"),
        P(None, "ctx", "head", None),
        P(None, "ctx", "head", None),
        P(None, "head", "ctx"),
    )
    return jax.shard_map(
        functools.partial(body, chips, ranks),
        mesh=mesh,
        in_specs=in_specs,
        out_specs=out_specs,
        check_vma=False,
    )
```

time: 1850 us -> 84.3 us (0.05)
  the two profiles are of different devices: /device:TPU:95 before, /device:TPU:1 now
where the time goes in v1:
time: 84.3 us; the launch traced here: 83.9 us
  Pallas kernels  74.5 us (88%)
  local copies, waits for them, and re-layouts  8.7 us (10%)
    pallas_call x1, Pallas kernels, body(): pl.pallas_call(functools.partial(kernel, chips, ranks, float(wide * ranks...  74.5 us
    unnamed x22, local copies, waits for them, and re-layouts  8.7 us

profile of v1, /device:TPU:1, one launch (start us, length us, event | category | flops | bytes accessed | tf_op | source)
XLA Modules:
  0.0 83.9 jit_solution(5761797224575017354)
XLA Ops:
  0.6 0.0 copy-start.6
  0.6 0.0 copy-start.7
  0.7 0.0 copy-start.8
  0.7 0.7 copy-done.6
  1.3 0.0 copy-done.7
  1.3 0.0 copy-done.8
  1.3 0.0 copy-start
  1.3 1.0 %copy-done = bf16[256,1024]{1,0:T(8,128)(2,1)S(1)} copy-done((bf16[256,1024]{1,0:T(8,128)(2,1)S(1)}, bf16[256,1024]{1,0:T(8,128)(2,1)}, u32[]{:S(2)}) %copy-start) | copy-done | bytes 524312
  2.4 0.0 copy-start.1
  2.4 1.0 %copy-done.1 = bf16[256,1024]{1,0:T(8,128)(2,1)S(1)} copy-done((bf16[256,1024]{1,0:T(8,128)(2,1)S(1)}, bf16[256,1024]{1,0:T(8,128)(2,1)}, u32[]{:S(2)}) %copy-start.1) | copy-done | bytes 524312
  3.4 0.0 copy-start.2
  3.4 0.8 copy-done.2
  4.3 0.0 copy-start.3
  4.3 0.8 copy-done.3
  5.1 0.0 copy-start.4
  5.1 0.7 copy-done.4
  5.8 0.0 copy-start.5
  5.8 0.7 copy-done.5
  6.5 74.5 %layer.1 = (f32[256,1024]{1,0:T(8,128)S(1)}, f32[256,128]{1,0:T(8,128)S(1)}, f32[256,128]{1,0:T(8,128)S(1)}, f32[8,256]{1,0:T(8,128)S(1)}) custom-call(bf16[256,1024]{1,0:T(8,128)(2,1)S(1)} %copy-done, bf16[256,1024]{1,0:T(8,128)(2,1)S(1)} %copy-done.1, bf16[256,128]{1,0:T(8,128)(2,1)S(1)} %bitcast.13, bf16[256,128]{1,0:T(8,128)(2,1)S(1)} %bitcast.14, ...), custom_call_target="tpu_custom_call" | custom-call | tf_op jit(solution)/shard_map/layer/pallas_call | solution.py:487
  81.0 1.0 %copy.19 = f32[256,1024]{1,0:T(8,128)} copy(f32[256,1024]{1,0:T(8,128)S(1)} %get-tuple-element.20) | data formatting | bytes 2097152
  82.0 0.7 copy.20
  82.6 0.7 copy.21
  83.3 0.6 copy.22
Async XLA Ops:
  0.6 0.7 copy-start.6
  0.6 0.7 copy-start.7
  0.7 0.7 copy-start.8
  1.3 1.0 %copy-start = (bf16[256,1024]{1,0:T(8,128)(2,1)S(1)}, bf16[256,1024]{1,0:T(8,128)(2,1)}, u32[]{:S(2)}) copy-start(bf16[256,1024]{1,0:T(8,128)(2,1)} %x_ref.1) | copy-start | bytes 1572868
  2.4 1.0 %copy-start.1 = (bf16[256,1024]{1,0:T(8,128)(2,1)S(1)}, bf16[256,1024]{1,0:T(8,128)(2,1)}, u32[]{:S(2)}) copy-start(bf16[256,1024]{1,0:T(8,128)(2,1)} %target_ref.1) | copy-start | bytes 1572868
  3.4 0.8 %copy-start.2 = (bf16[1,256,1,128]{3,1,2,0:T(8,128)(2,1)S(1)}, bf16[1,256,1,128]{3,1,2,0:T(8,128)(2,1)}, u32[]{:S(2)}) copy-start(bf16[1,256,1,128]{3,1,2,0:T(8,128)(2,1)} %param.10) | copy-start | bytes 196612
  4.3 0.8 %copy-start.3 = (bf16[1,256,1,128]{3,1,2,0:T(8,128)(2,1)S(1)}, bf16[1,256,1,128]{3,1,2,0:T(8,128)(2,1)}, u32[]{:S(2)}) copy-start(bf16[1,256,1,128]{3,1,2,0:T(8,128)(2,1)} %param.11) | copy-start | bytes 196612
  5.1 0.7 copy-start.4
  5.8 0.7 copy-start.5

commit v2 on v1

v2 whole, which is shorter than its diff:
```python
import functools

import jax
import jax.numpy as jnp
from jax import lax
from jax.experimental import pallas as pl
from jax.experimental.pallas import tpu as pltpu
from jax.sharding import PartitionSpec as P

EPSILON = 1e-05
MESH = pl.DeviceIdType.MESH
F32 = jnp.float32
BF16 = jnp.bfloat16
NN = (((1,), (0,)), ((), ()))
NT = (((1,), (1,)), ((), ()))

CUM, EXPCUM, ENDW, ENDDEC, STEP = range(5)


def mm(left, right, dims=NN):
    return lax.dot_general(left, right, dims, preferred_element_type=F32)


def split2(value):
    high = value.astype(BF16)
    low = (value - high.astype(F32)).astype(BF16)
    return high, low


def split3(value):
    high = value.astype(BF16)
    rest = value - high.astype(F32)
    mid = rest.astype(BF16)
    low = (rest - mid.astype(F32)).astype(BF16)
    return high, mid, low


def mm3(left, right, dims=NN):
    (lh, ll), (rh, rl) = left, right
    return mm(lh, rh, dims) + (mm(lh, rl, dims) + mm(ll, rh, dims))


def kernel(
    chips,
    ranks,
    width,
    x_hbm,
    target_hbm,
    b_hbm,
    c_hbm,
    step_hbm,
    forget_hbm,
    rate_hbm,
    skip_hbm,
    gain_hbm,
    gx_ref,
    gb_ref,
    gc_ref,
    gs_ref,
    x_ref,
    target_ref,
    b_ref,
    c_ref,
    step_ref,
    forget_ref,
    rate_ref,
    skip_ref,
    gain_ref,
    rows_ref,
    cols_ref,
    ends_ref,
    skips_ref,
    scores_ref,
    mixed_ref,
    gm_ref,
    y_ref,
    rq_ref,
    ext_ref,
    sin_ref,
    gout_ref,
    btr_ref,
    ctr_ref,
    dst_ref,
    sum_ref,
    fl_own,
    fl_got,
    fm_out,
    fm_in,
    fp_out,
    fp_in,
    fs_out,
    fs_in,
    bl_own,
    bl_got,
    bm_out,
    bm_in,
    bp_out,
    bp_in,
    bs_out,
    bs_in,
    z_out,
    z_in,
    load_sem,
    pair_send,
    pair_recv,
    ring_send,
    ring_recv,
    z_send,
    z_recv,
):
    tokens = x_ref.shape[0]
    heads = step_ref.shape[0]
    half = heads // 2
    chan = x_ref.shape[1] // heads
    parts, pair = 2, half // 2
    piece = pair * 128 // chips
    per_head = chips // pair
    ctx = lax.axis_index("ctx")
    rank = lax.axis_index("head")
    chip, core = lax.div(ctx, 2), lax.rem(ctx, 2)
    sibling = (chip * 2 + 1 - core, rank)
    lines = chips // 4
    line, place = lax.div(chip, 4), lax.rem(chip, 4)

    loads = [
        pltpu.make_async_copy(source, target, load_sem.at[i])
        for i, (source, target) in enumerate(
            (
                (step_hbm, step_ref),
                (forget_hbm, forget_ref),
                (rate_hbm, rate_ref),
                (b_hbm, b_ref),
                (x_hbm, x_ref),
                (c_hbm, c_ref),
                (skip_hbm, skip_ref),
                (gain_hbm, gain_ref),
                (target_hbm, target_ref),
            )
        )
    ]
    for load in loads:
        load.start()

    def loop(low, high, step):
        def turn(i, carry):
            step(i)
            return carry

        lax.fori_loop(low, high, turn, 0)

    def other_chips(act):
        columns = [lax.rem(place + along, 4) for along in (2, 1, 3, 0)]

        def on_line(q, count):
            down = lines // 2 + (1 - 2 * lax.rem(q, 2)) * lax.div(q + 1, 2)
            base = lax.rem(line + down, lines) * 4
            for column in columns[:count]:
                act(base + column)

        if lines > 1:
            loop(0, lines - 1, lambda q: on_line(q, 4))
        on_line(jnp.int32(lines - 1), 3)

    def other_ranks(act):
        for away in sorted(range(1, ranks), key=lambda k: -min(k, ranks - k)):
            act(lax.rem(rank + away, ranks))

    barrier = pltpu.get_barrier_semaphore()

    def greet(device):
        pl.semaphore_signal(barrier, inc=1, device_id=device, device_id_type=MESH)

    other_chips(lambda other: greet((other * 2 + core, rank)))
    other_ranks(lambda other: greet((ctx, other)))
    greet(sibling)

    down_iota = lax.broadcasted_iota(jnp.int32, (tokens, tokens), 0)
    along_iota = lax.broadcasted_iota(jnp.int32, (tokens, tokens), 1)
    diagonal = down_iota[0:heads, 0:heads] == along_iota[0:heads, 0:heads]

    def as_column(row):
        return jnp.sum(jnp.where(diagonal, row, 0.0), axis=1, keepdims=True)

    for load in loads[0:3]:
        load.wait()
    rate = jnp.exp(as_column(rate_ref[...]))
    step = step_ref[...]
    logdec = -step * rate - forget_ref[...]
    upper = (down_iota <= along_iota).astype(F32).astype(BF16)
    high, mid, low = split3(logdec)
    cum = mm(high, upper) + (mm(mid, upper) + mm(low, upper))
    last = cum[:, tokens - 1 : tokens]
    expcum = jnp.exp(cum)
    enddec = jnp.exp(last - cum)
    table = [cum, expcum, enddec * step, enddec, step]
    rows_ref[0] = cum
    rows_ref[1] = step
    ends_ref[...] = jnp.broadcast_to(jnp.exp(last), (heads, 128))
    table = jnp.concatenate(table + [jnp.zeros((128 - heads * len(table), tokens), F32)], axis=0)
    cols_ref[...] = table.T
    loads[3].wait()
    btr_ref[...] = b_ref[...].astype(F32).T.astype(BF16)
    loads[4].wait()

    def columns_of(h):
        rolled = pltpu.roll(cols_ref[...], lax.rem(128 - h, 128), 1)
        return [rolled[:, 8 * q : 8 * q + 1] for q in range(5)]

    def channels(h):
        return pl.ds(pl.multiple_of(h * chan, chan), chan)

    def cum_row(h):
        return rows_ref[0, pl.ds(h, 1), :]

    def step_row(h):
        return rows_ref[1, pl.ds(h, 1), :]

    def decay_of(h):
        return ends_ref[pl.ds(h, 1), :]

    def skip_of(h):
        return skips_ref[pl.ds(h, 1), :]

    def local_state(h):
        weighted = x_ref[:, channels(h)].astype(F32) * columns_of(h)[ENDW]
        high, low = split2(weighted)
        fl_own[h, 0:128, :] = mm(btr_ref[...], high) + mm(btr_ref[...], low)
        fl_own[h, 128:136, :] = jnp.broadcast_to(decay_of(h), (8, 128))

    def to_sibling(source, target, sem):
        return pltpu.make_async_remote_copy(
            src_ref=source,
            dst_ref=target,
            send_sem=pair_send.at[sem],
            recv_sem=pair_recv.at[sem],
            device_id=sibling,
            device_id_type=MESH,
        )

    mine, theirs = core * half, (1 - core) * half

    def swap_of(own, got, part, sem):
        return to_sibling(own.at[pl.ds(theirs + part * pair, pair)], got.at[pl.ds(part * pair, pair)], sem)

    def heads_of(base, part, act):
        loop(0, pair, lambda i: act(base + part * pair + i))

    def ring_start(source, target, part, rows_sent, sem):
        def start(other):
            pltpu.make_async_remote_copy(
                src_ref=source.at[part, other, 0:rows_sent],
                dst_ref=target.at[part, chip, 0:rows_sent],
                send_sem=ring_send.at[sem],
                recv_sem=ring_recv.at[sem],
                device_id=(other * 2 + core, rank),
                device_id_type=MESH,
            ).start()

        other_chips(start)
        target[part, chip, 0:rows_sent, :] = source[part, chip, 0:rows_sent, :]

    def ring_all(source, target, part, rows_sent, sem):
        return pltpu.make_async_remote_copy(
            src_ref=source.at[part, 0 : chips - 1, 0:rows_sent],
            dst_ref=target.at[part, 0 : chips - 1, 0:rows_sent],
            send_sem=ring_send.at[sem],
            recv_sem=ring_recv.at[sem],
            device_id=sibling,
            device_id_type=MESH,
        )

    def pair_of(own, got, i):
        own_rows, got_rows = own[mine + i, 0:128, :], got[i, 0:128, :]
        first = jnp.where(core == 0, own_rows, got_rows)
        second = jnp.where(core == 0, got_rows, own_rows)
        return first, second

    def decay_pair(i):
        own_decay, got_decay = fl_own[mine + i, 128:129, :], fl_got[i, 128:129, :]
        first = jnp.where(core == 0, own_decay, got_decay)
        second = jnp.where(core == 0, got_decay, own_decay)
        return first, second

    def owners_of(part, i):
        return part, pl.ds(i * per_head, per_head), pl.ds(0, piece)

    def join_forward(part):
        for i in range(pair):
            first, second = pair_of(fl_own, fl_got, part * pair + i)
            decay0, decay1 = decay_pair(part * pair + i)
            joined = decay1 * first + second
            fm_out[owners_of(part, i)] = joined.reshape(per_head, piece, 128)
            fm_out[part, pl.ds(i * per_head, per_head), pl.ds(piece, 8)] = jnp.broadcast_to(
                (decay0 * decay1)[None], (per_head, 8, 128)
            )

    for part in range(parts):
        heads_of(theirs, part, local_state)
        if part == 0:
            pl.semaphore_wait(barrier, (chips - 1) + (ranks - 1) + 1)
        swap_of(fl_own, fl_got, part, part).start()
    for part in range(parts):
        heads_of(mine, part, local_state)
        swap_of(fl_own, fl_got, part, part).wait_recv()
        join_forward(part)
        ring_start(fm_out, fm_in, part, piece + 1, part)

    for load in loads[5:]:
        load.wait()
    skips_ref[...] = jnp.broadcast_to(as_column(skip_ref[...]), (heads, 128))
    ctr_ref[...] = c_ref[...].astype(F32).T.astype(BF16)
    scores_ref[...] = mm(c_ref[...], b_ref[...], NT)

    def near(h):
        cols = columns_of(h)
        gap = jnp.where(down_iota >= along_iota, cols[CUM] - cum_row(h), -1e30)
        weights = scores_ref[...] * jnp.exp(gap) * step_row(h)
        high, low = split2(weights)
        x_h = x_ref[:, channels(h)]
        mixed_ref[:, channels(h)] = mm(high, x_h) + mm(low, x_h)

    loop(0, heads, near)
    sum_ref[...] = jnp.zeros_like(sum_ref)

    for part in range(parts):
        ring_all(fm_out, fm_in, part, piece + 1, part).wait_recv()
        state = jnp.zeros((piece, 128), F32)
        for t in range(chips):
            fp_out[part, t] = state
            state = fm_in[part, t, piece : piece + 1, :] * state + fm_in[part, t, 0:piece, :]
        ring_start(fp_out, fp_in, part, piece, 2 + part)

    def enter(part):
        for i in range(pair):
            at = part * pair + i
            first, _ = pair_of(fl_own, fl_got, at)
            decay0, _ = decay_pair(at)
            for_first = fp_in[owners_of(part, i)].reshape(128, 128)
            for_second = decay0 * for_first + first
            sin_ref[mine + at] = jnp.where(core == 0, for_first, for_second)
            fs_out[at] = jnp.where(core == 0, for_second, for_first)

    def both(own, got, part, sem):
        here = pl.ds(part * pair, pair)
        return to_sibling(own.at[here], got.at[here], sem)

    def far(h):
        cols = columns_of(h)
        high, low = split2(sin_ref[h])
        reached = mm(c_ref[...], high) + mm(c_ref[...], low)
        x_h = x_ref[:, channels(h)].astype(F32)
        mixed = mixed_ref[:, channels(h)] + cols[EXPCUM] * reached + skip_of(h) * x_h
        mixed_ref[:, channels(h)] = mixed
        gained = gain_ref[:, channels(h)] * mixed
        sum_ref[0] += mixed * mixed
        sum_ref[1] += gained * (x_h - target_ref[:, channels(h)].astype(F32))
        sum_ref[2] += gained * gained

    for part in range(parts):
        ring_all(fp_out, fp_in, part, piece, 2 + part).wait_recv()
        enter(part)
        both(fs_out, fs_in, part, 2 + part).start()
        heads_of(mine, part, far)
    for part in range(parts):
        both(fs_out, fs_in, part, 2 + part).wait_recv()
        for i in range(pair):
            sin_ref[theirs + part * pair + i] = fs_in[part * pair + i]
        heads_of(theirs, part, far)

    lane = lax.broadcasted_iota(jnp.int32, (tokens, 128), 1)
    packed = jnp.zeros((tokens, 128), F32)
    for i in range(3):
        packed = jnp.where(lane == i, jnp.sum(sum_ref[i], axis=1, keepdims=True), packed)
    z_out[...] = packed.T[0:8, :]

    def z_copy(to, slot):
        return pltpu.make_async_remote_copy(
            src_ref=z_out,
            dst_ref=z_in.at[slot],
            send_sem=z_send.at[to],
            recv_sem=z_recv.at[slot],
            device_id=(ctx, to),
            device_id_type=MESH,
        )

    other_ranks(lambda other: z_copy(other, rank).start())
    z_in[rank] = z_out[...]
    other_ranks(lambda other: z_copy(other, other).wait_recv())
    total = z_in[0]
    for i in range(1, ranks):
        total = total + z_in[i]
    inv_scale = lax.rsqrt(total[0:1, :] / width + EPSILON)
    inner = total[1:2, :] + inv_scale * total[2:3, :]
    coef = inner * inv_scale * inv_scale * inv_scale / width
    back = jnp.concatenate([inv_scale, coef, jnp.zeros((126, tokens), F32)], axis=0).T
    inv_col, coef_col = back[:, 0:1], back[:, 1:2]

    def norm_back(h):
        gain = gain_ref[:, channels(h)]
        mixed = mixed_ref[:, channels(h)]
        x_h = x_ref[:, channels(h)].astype(F32)
        grad_out = x_h + gain * mixed * inv_col - target_ref[:, channels(h)].astype(F32)
        grad_mixed = gain * grad_out * inv_col - mixed * coef_col
        gm_ref[:, channels(h)] = grad_mixed
        gx_ref[:, channels(h)] = grad_out + skip_of(h) * grad_mixed
        high, low = split2(grad_mixed * columns_of(h)[EXPCUM])
        bl_own[h] = mm(ctr_ref[...], high) + mm(ctr_ref[...], low)

    def join_back(part):
        for i in range(pair):
            first, second = pair_of(bl_own, bl_got, part * pair + i)
            decay0, _ = decay_pair(part * pair + i)
            bm_out[owners_of(part, i)] = (decay0 * second + first).reshape(per_head, piece, 128)

    for part in range(parts):
        heads_of(theirs, part, norm_back)
        swap_of(bl_own, bl_got, part, 4 + part).start()
    for part in range(parts):
        heads_of(mine, part, norm_back)
        swap_of(bl_own, bl_got, part, 4 + part).wait_recv()
        join_back(part)
        ring_start(bm_out, bm_in, part, piece, 4 + part)

    rq_ref[...] = jnp.zeros_like(rq_ref)
    gc_ref[...] = jnp.zeros_like(gc_ref)
    gb_ref[...] = jnp.zeros_like(gb_ref)
    dst_ref[...] = jnp.zeros_like(dst_ref)
    scores_ref[...] = mm(b_ref[...], c_ref[...], NT)

    def near_back(h):
        cols = columns_of(h)
        gap = jnp.where(along_iota >= down_iota, cum_row(h) - cols[CUM], -1e30)
        decay = jnp.exp(gap)
        grad_mixed = gm_ref[:, channels(h)]
        gm_parts = split2(grad_mixed)
        x_h = x_ref[:, channels(h)]
        y_ref[:, channels(h)] = mm3(split2(scores_ref[...] * decay), gm_parts)
        grad_weights = mm(x_h, gm_parts[0], NT) + mm(x_h, gm_parts[1], NT)
        dst_ref[...] += grad_weights * decay * cols[STEP]
        own = grad_mixed * (mixed_ref[:, channels(h)] - skip_of(h) * x_h.astype(F32))
        rq_ref[...] = jnp.where(lane == h, jnp.sum(own, axis=1, keepdims=True), rq_ref[...])
        gc_ref[...] += mm3(split2(grad_mixed * cols[EXPCUM]), split2(sin_ref[h]), NT)

    loop(0, heads, near_back)
    grad_scores = dst_ref[...]
    high, low = split2(grad_scores)
    gb_ref[...] += mm(high, c_ref[...]) + mm(low, c_ref[...])
    high, low = split2(grad_scores.T)
    gc_ref[...] += mm(high, b_ref[...]) + mm(low, b_ref[...])

    for part in range(parts):
        ring_all(bm_out, bm_in, part, piece, 4 + part).wait_recv()
        grad = jnp.zeros((piece, 128), F32)
        for t in reversed(range(chips)):
            bp_out[part, t] = grad
            grad = fm_in[part, t, piece : piece + 1, :] * grad + bm_in[part, t]
        ring_start(bp_out, bp_in, part, piece, 6 + part)

    def leave(part):
        for i in range(pair):
            at = part * pair + i
            _, second = pair_of(bl_own, bl_got, at)
            _, decay1 = decay_pair(at)
            for_second = bp_in[owners_of(part, i)].reshape(128, 128)
            for_first = decay1 * for_second + second
            gout_ref[mine + at] = jnp.where(core == 0, for_first, for_second)
            bs_out[at] = jnp.where(core == 0, for_second, for_first)

    def far_back(h):
        cols = columns_of(h)
        grad_state = gout_ref[h]
        high, low = split2(grad_state)
        x_h = x_ref[:, channels(h)]
        reached = mm(b_ref[...], high) + mm(b_ref[...], low)
        value = y_ref[:, channels(h)] + cols[ENDDEC] * reached
        gx_ref[:, channels(h)] += cols[STEP] * value
        own = jnp.sum(x_h.astype(F32) * value, axis=1, keepdims=True)
        rq_ref[...] = jnp.where(lane == h + 8, own, rq_ref[...])
        gb_ref[...] += cols[ENDW] * (mm(x_h, high, NT) + mm(x_h, low, NT))
        leaving = decay_of(h) * sin_ref[h] + fl_own[h, 0:128, :]
        ext_ref[pl.ds(h, 1), :] = jnp.sum(grad_state * leaving, axis=0, keepdims=True)

    for part in range(parts):
        ring_all(bp_out, bp_in, part, piece, 6 + part).wait_recv()
        leave(part)
        both(bs_out, bs_in, part, 6 + part).start()
        heads_of(mine, part, far_back)
    for part in range(parts):
        both(bs_out, bs_in, part, 6 + part).wait_recv()
        for i in range(pair):
            gout_ref[theirs + part * pair + i] = bs_in[part * pair + i]
        heads_of(theirs, part, far_back)

    ends = rq_ref[...].T
    inner_x = ends[8 : 8 + heads, :]
    extra = jnp.sum(ext_ref[...], axis=1, keepdims=True)
    token_iota = lax.broadcasted_iota(jnp.int32, (heads, tokens), 1)
    grad_cum = ends[0:heads, :] - step * inner_x + jnp.where(token_iota == tokens - 1, extra, 0.0)
    lower = (down_iota >= along_iota).astype(F32).astype(BF16)
    high, mid, low = split3(grad_cum)
    grad_dec = mm(high, lower) + (mm(mid, lower) + mm(low, lower))
    gs_ref[...] = inner_x - rate * grad_dec

    for part in range(parts):
        swap_of(fl_own, fl_got, part, part).wait_send()
        both(fs_out, fs_in, part, 2 + part).wait_send()
        swap_of(bl_own, bl_got, part, 4 + part).wait_send()
        both(bs_out, bs_in, part, 6 + part).wait_send()
        ring_all(fm_out, fm_in, part, piece + 1, part).wait_send()
        ring_all(fp_out, fp_in, part, piece, 2 + part).wait_send()
        ring_all(bm_out, bm_in, part, piece, 4 + part).wait_send()
        ring_all(bp_out, bp_in, part, piece, 6 + part).wait_send()
    other_ranks(lambda other: z_copy(other, other).wait_send())


def copy_out(*refs):
    count = len(refs) // 2
    sources, targets, sems = refs[:count], refs[count:-1], refs[-1]
    copies = [pltpu.make_async_copy(s, t, sems.at[i]) for i, (s, t) in enumerate(zip(sources, targets))]
    for copy in copies:
        copy.start()
    for copy in copies:
        copy.wait()


def body(chips, ranks, inputs, b_proj, c_proj, step_sizes, log_rate, forget, skip_gain, norm_gain, target):
    tokens, wide = inputs.shape
    heads = step_sizes.shape[1]
    half = heads // 2
    piece = half * 64 // chips
    vmem = pl.BlockSpec(memory_space=pltpu.VMEM)
    hbm = pl.BlockSpec(memory_space=pltpu.HBM)

    def buffer(*shape, dtype=F32):
        return pltpu.VMEM(shape, dtype)

    state = (heads, 128, 128)
    half_state = (half, 128, 128)
    operands = (
        inputs,
        target,
        b_proj.reshape(tokens, 128),
        c_proj.reshape(tokens, 128),
        step_sizes[0],
        forget[0],
        log_rate,
        skip_gain,
        norm_gain,
    )
    out_shape = (
        jax.ShapeDtypeStruct((tokens, wide), F32),
        jax.ShapeDtypeStruct((tokens, 128), F32),
        jax.ShapeDtypeStruct((tokens, 128), F32),
        jax.ShapeDtypeStruct((heads, tokens), F32),
    )
    results = pl.pallas_call(
        functools.partial(kernel, chips, ranks, float(wide * ranks)),
        out_shape=out_shape,
        in_specs=[hbm] * len(operands),
        out_specs=[vmem] * 4,
        scratch_shapes=[buffer(*operand.shape, dtype=operand.dtype) for operand in operands]
        + [
            buffer(2, heads, tokens),
            buffer(tokens, 128),
            buffer(heads, 128),
            buffer(heads, 128),
            buffer(tokens, tokens),
            buffer(tokens, wide),
            buffer(tokens, wide),
            buffer(tokens, wide),
            buffer(tokens, 128),
            buffer(heads, 128),
            buffer(*state),
            buffer(*state),
            buffer(128, tokens, dtype=BF16),
            buffer(128, tokens, dtype=BF16),
            buffer(tokens, tokens),
            buffer(3, tokens, 128),
            buffer(heads, 136, 128),
            buffer(half, 136, 128),
            buffer(2, chips, piece + 8, 128),
            buffer(2, chips, piece + 8, 128),
            buffer(2, chips, piece, 128),
            buffer(2, chips, piece, 128),
            buffer(*half_state),
            buffer(*half_state),
            buffer(*state),
            buffer(*half_state),
            buffer(2, chips, piece, 128),
            buffer(2, chips, piece, 128),
            buffer(2, chips, piece, 128),
            buffer(2, chips, piece, 128),
            buffer(*half_state),
            buffer(*half_state),
            buffer(8, tokens),
            buffer(ranks, 8, tokens),
            pltpu.SemaphoreType.DMA((9,)),
            pltpu.SemaphoreType.DMA((8,)),
            pltpu.SemaphoreType.DMA((8,)),
            pltpu.SemaphoreType.DMA((8,)),
            pltpu.SemaphoreType.DMA((8,)),
            pltpu.SemaphoreType.DMA((ranks,)),
            pltpu.SemaphoreType.DMA((ranks,)),
        ],
        compiler_params=pltpu.CompilerParams(
            collective_id=0, has_side_effects=True, vmem_limit_bytes=24 * 1024 * 1024
        ),
        name="layer",
    )(*operands)
    grad_x, grad_b, grad_c, grad_steps = pl.pallas_call(
        copy_out,
        out_shape=out_shape,
        in_specs=[pl.BlockSpec(memory_space=pl.ANY)] * 4,
        out_specs=[hbm] * 4,
        scratch_shapes=[pltpu.SemaphoreType.DMA((4,))],
        name="copy_out",
    )(*results)
    return (
        grad_x,
        grad_b.reshape(1, tokens, 1, 128),
        grad_c.reshape(1, tokens, 1, 128),
        grad_steps[None],
    )


def solution(mesh):
    chips, ranks = mesh.shape["ctx"] // 2, mesh.shape["head"]
    in_specs = (
        P("ctx", "head"),
        P(None, "ctx", "head", None),
        P(None, "ctx", "head", None),
        P(None, "head", "ctx"),
        P(None, "head"),
        P(None, "head", "ctx"),
        P(None, "head"),
        P(None, "head"),
        P("ctx", "head"),
    )
    out_specs = (
        P("ctx", "head"),
        P(None, "ctx", "head", None),
        P(None, "ctx", "head", None),
        P(None, "head", "ctx"),
    )
    return jax.shard_map(
        functools.partial(body, chips, ranks),
        mesh=mesh,
        in_specs=in_specs,
        out_specs=out_specs,
        check_vma=False,
    )
```

time: 84.3 us -> 113 us (1.34)
  Pallas kernels: 74.5 us -> 103 us
    pallas_call x0 -> x1, Pallas kernels: none -> 41.1 us  [body(): pl.pallas_call(copy_out, out_shape=out_shape, in_specs=[pl.BlockSpec(memo...]
    pallas_call x1, Pallas kernels: 74.5 us -> 62.3 us  [body(): pl.pallas_call(functools.partial(kernel, chips, ranks, float(wide * ranks...]
    unnamed x22 -> x26, local copies, waits for them, and re-layouts: 8.7 us -> 8.7 us
where the time goes in v2:
time: 113 us
  Pallas kernels  103 us (91%)
  local copies, waits for them, and re-layouts  8.7 us (8%)
    pallas_call x1, Pallas kernels, body(): pl.pallas_call(functools.partial(kernel, chips, ranks, float(wide * ranks...  62.3 us
    pallas_call x1, Pallas kernels, body(): pl.pallas_call(copy_out, out_shape=out_shape, in_specs=[pl.BlockSpec(memo...  41.1 us
    unnamed x26, local copies, waits for them, and re-layouts  8.7 us

profile of v2, /device:TPU:1, one launch (start us, length us, event | category | flops | bytes accessed | tf_op | source)
XLA Modules:
  0.0 112.8 jit_solution(12039929328786214025)
XLA Ops:
  0.6 0.0 copy-start.10
  0.6 0.0 copy-start.11
  0.7 0.0 copy-start.12
  0.7 0.7 copy-done.10
  1.3 0.0 copy-done.11
  1.3 0.0 copy-done.12
  1.3 0.0 copy-start.1
  1.3 1.0 copy-done.1
  2.4 0.0 copy-start.2
  2.4 1.0 copy-done.2
  3.4 0.0 copy-start.5
  3.4 0.8 copy-done.5
  4.3 0.0 copy-start.6
  4.3 0.8 copy-done.6
  5.1 0.0 copy-start.7
  5.1 0.7 copy-done.7
  5.8 0.0 copy-start.8
  5.8 0.7 copy-done.8
  6.5 62.3 %layer.1 = (f32[256,1024]{1,0:T(8,128)S(1)}, f32[256,128]{1,0:T(8,128)S(1)}, f32[256,128]{1,0:T(8,128)S(1)}, f32[8,256]{1,0:T(8,128)S(1)}) custom-call(bf16[256,1024]{1,0:T(8,128)(2,1)S(1)} %copy-done.1, bf16[256,1024]{1,0:T(8,128)(2,1)S(1)} %copy-done.2, bf16[256,128]{1,0:T(8,128)(2,1)S(1)} %bitcast.11, bf16[256,128]{1,0:T(8,128)(2,1)S(1)} %bitcast.12, ...), custom_call_target="tpu_custom_call" | custom-call | tf_op jit(solution)/shard_map/layer/pallas_call | solution.py:556
  68.8 0.0 copy-start
  68.8 1.0 copy-done
  69.8 0.0 copy-start.3
  69.8 0.6 copy-done.3
  70.4 0.0 copy-start.4
  70.4 0.7 copy-done.4
  71.1 0.0 copy-start.9
  71.1 0.6 copy-done.9
  71.7 41.1 %copy_out.1 = (f32[256,1024]{1,0:T(8,128)}, f32[256,128]{1,0:T(8,128)}, f32[256,128]{1,0:T(8,128)}, f32[8,256]{1,0:T(8,128)}) custom-call(f32[256,1024]{1,0:T(8,128)} %copy-done, f32[256,128]{1,0:T(8,128)} %copy-done.3, f32[256,128]{1,0:T(8,128)} %copy-done.4, f32[8,256]{1,0:T(8,128)} %copy-done.9), custom_call_target="tpu_custom_call" | custom-call | tf_op jit(solution)/shard_map/copy_out/pallas_call | solution.py:610
Async XLA Ops:
  0.6 0.7 copy-start.10
  0.6 0.7 copy-start.11
  0.7 0.7 copy-start.12
  1.3 1.0 copy-start.1
  2.4 1.0 copy-start.2
  3.4 0.8 copy-start.5
  4.3 0.8 copy-start.6
  5.1 0.7 copy-start.7
  5.8 0.7 copy-start.8
  68.8 1.0 copy-start
  69.8 0.7 copy-start.3
  70.4 0.7 copy-start.4
  71.1 0.6 copy-start.9

commit v3 on v2

--- a/solution.py
+++ b/solution.py
@@ -547,6 +547,7 @@
         skip_gain,
         norm_gain,
     )
+    operands = tuple(pltpu.with_memory_space_constraint(operand, pltpu.HBM) for operand in operands)
     out_shape = (
         jax.ShapeDtypeStruct((tokens, wide), F32),
         jax.ShapeDtypeStruct((tokens, 128), F32),
@@ -613,6 +614,7 @@
         in_specs=[pl.BlockSpec(memory_space=pl.ANY)] * 4,
         out_specs=[hbm] * 4,
         scratch_shapes=[pltpu.SemaphoreType.DMA((4,))],
+        compiler_params=pltpu.CompilerParams(vmem_limit_bytes=1024 * 1024),
         name="copy_out",
     )(*results)
     return (

time: 113 us -> 64.3 us (0.57)
  Pallas kernels: 103 us -> 63.5 us
  local copies, waits for them, and re-layouts: 8.7 us -> 0 us
    pallas_call x1, Pallas kernels: 41.1 us -> 1.08 us  [body(): pl.pallas_call(copy_out, out_shape=out_shape, in_specs=[pl.BlockSpec(memo...]
    unnamed x26 -> x0, local copies, waits for them, and re-layouts: 8.7 us -> none
where the time goes in v3:
time: 64.3 us; the launch traced here: 64.2 us
  Pallas kernels  63.5 us (99%)
    pallas_call x1, Pallas kernels, body(): pl.pallas_call(functools.partial(kernel, chips, ranks, float(wide * ranks...  62.5 us

profile of v3, /device:TPU:1, one launch (start us, length us, event | category | flops | bytes accessed | tf_op | source)
XLA Modules:
  0.0 64.2 jit_solution(16236402455423243555)
XLA Ops:
  0.6 62.5 %layer.1 = (f32[256,1024]{1,0:T(8,128)S(1)}, f32[256,128]{1,0:T(8,128)S(1)}, f32[256,128]{1,0:T(8,128)S(1)}, f32[8,256]{1,0:T(8,128)S(1)}) custom-call(bf16[256,1024]{1,0:T(8,128)(2,1)} %x_hbm.1, bf16[256,1024]{1,0:T(8,128)(2,1)} %target_hbm.1, bf16[256,128]{1,0:T(8,128)(2,1)} %bitcast.11, bf16[256,128]{1,0:T(8,128)(2,1)} %bitcast.12, f32[8,256]{1,0:T(8,128)} %bitcast.13, ...), custom_call_target="tpu_custom_call" | custom-call | tf_op jit(solution)/shard_map/layer/pallas_call | solution.py:557
  63.1 1.1 %copy_out.1 = (f32[256,1024]{1,0:T(8,128)}, f32[256,128]{1,0:T(8,128)}, f32[256,128]{1,0:T(8,128)}, f32[8,256]{1,0:T(8,128)}) custom-call(f32[256,1024]{1,0:T(8,128)S(1)} %get-tuple-element.12.refs_0_, f32[256,128]{1,0:T(8,128)S(1)} %get-tuple-element.13.refs_1_, f32[256,128]{1,0:T(8,128)S(1)} %get-tuple-element.14.refs_2_, ...), custom_call_target="tpu_custom_call" | custom-call | tf_op jit(solution)/shard_map/copy_out/pallas_call | solution.py:611

commit v4 on v3

--- a/solution.py
+++ b/solution.py
@@ -73,7 +73,12 @@
     scores_ref,
     mixed_ref,
     gm_ref,
-    y_ref,
+    u_ref,
+    expb_ref,
+    endwb_ref,
+    cc_ref,
+    bb_ref,
+    scale_ref,
     rq_ref,
     ext_ref,
     sin_ref,
@@ -122,6 +127,39 @@
     lines = chips // 4
     line, place = lax.div(chip, 4), lax.rem(chip, 4)
 
+    def loop(low, high, step):
+        def turn(i, carry):
+            step(i)
+            return carry
+
+        lax.fori_loop(low, high, turn, 0)
+
+    def other_chips(act):
+        columns = [lax.rem(place + along, 4) for along in (2, 1, 3, 0)]
+
+        def on_line(q, count):
+            down = lines // 2 + (1 - 2 * lax.rem(q, 2)) * lax.div(q + 1, 2)
+            base = lax.rem(line + down, lines) * 4
+            for column in columns[:count]:
+                act(base + column)
+
+        if lines > 1:
+            loop(0, lines - 1, lambda q: on_line(q, 4))
+        on_line(jnp.int32(lines - 1), 3)
+
+    def other_ranks(act):
+        for away in sorted(range(1, ranks), key=lambda k: -min(k, ranks - k)):
+            act(lax.rem(rank + away, ranks))
+
+    barrier = pltpu.get_barrier_semaphore()
+
+    def greet(device):
+        pl.semaphore_signal(barrier, inc=1, device_id=device, device_id_type=MESH)
+
+    other_chips(lambda other: greet((other * 2 + core, rank)))
+    other_ranks(lambda other: greet((ctx, other)))
+    greet(sibling)
+
     loads = [
         pltpu.make_async_copy(source, target, load_sem.at[i])
         for i, (source, target) in enumerate(
@@ -141,39 +179,6 @@
     for load in loads:
         load.start()
 
-    def loop(low, high, step):
-        def turn(i, carry):
-            step(i)
-            return carry
-
-        lax.fori_loop(low, high, turn, 0)
-
-    def other_chips(act):
-        columns = [lax.rem(place + along, 4) for along in (2, 1, 3, 0)]
-
-        def on_line(q, count):
-            down = lines // 2 + (1 - 2 * lax.rem(q, 2)) * lax.div(q + 1, 2)
-            base = lax.rem(line + down, lines) * 4
-            for column in columns[:count]:
-                act(base + column)
-
-        if lines > 1:
-            loop(0, lines - 1, lambda q: on_line(q, 4))
-        on_line(jnp.int32(lines - 1), 3)
-
-    def other_ranks(act):
-        for away in sorted(range(1, ranks), key=lambda k: -min(k, ranks - k)):
-            act(lax.rem(rank + away, ranks))
-
-    barrier = pltpu.get_barrier_semaphore()
-
-    def greet(device):
-        pl.semaphore_signal(barrier, inc=1, device_id=device, device_id_type=MESH)
-
-    other_chips(lambda other: greet((other * 2 + core, rank)))
-    other_ranks(lambda other: greet((ctx, other)))
-    greet(sibling)
-
     down_iota = lax.broadcasted_iota(jnp.int32, (tokens, tokens), 0)
     along_iota = lax.broadcasted_iota(jnp.int32, (tokens, tokens), 1)
     diagonal = down_iota[0:heads, 0:heads] == along_iota[0:heads, 0:heads]
@@ -195,6 +200,7 @@
     table = [cum, expcum, enddec * step, enddec, step]
     rows_ref[0] = cum
     rows_ref[1] = step
+    rows_ref[2] = enddec
     ends_ref[...] = jnp.broadcast_to(jnp.exp(last), (heads, 128))
     table = jnp.concatenate(table + [jnp.zeros((128 - heads * len(table), tokens), F32)], axis=0)
     cols_ref[...] = table.T
@@ -202,9 +208,10 @@
     btr_ref[...] = b_ref[...].astype(F32).T.astype(BF16)
     loads[4].wait()
 
-    def columns_of(h):
+    def columns_of(h, count=1):
         rolled = pltpu.roll(cols_ref[...], lax.rem(128 - h, 128), 1)
-        return [rolled[:, 8 * q : 8 * q + 1] for q in range(5)]
+        each = [[rolled[:, 8 * q + k : 8 * q + k + 1] for q in range(5)] for k in range(count)]
+        return each if count > 1 else each[0]
 
     def channels(h):
         return pl.ds(pl.multiple_of(h * chan, chan), chan)
@@ -221,11 +228,17 @@
     def skip_of(h):
         return skips_ref[pl.ds(h, 1), :]
 
+    def two(make):
+        return jnp.concatenate([make(0), make(1)], axis=1)
+
     def local_state(h):
-        weighted = x_ref[:, channels(h)].astype(F32) * columns_of(h)[ENDW]
+        columns = columns_of(h, 2)
+        weighted = two(lambda k: x_ref[:, channels(h + k)].astype(F32) * columns[k][ENDW])
         high, low = split2(weighted)
-        fl_own[h, 0:128, :] = mm(btr_ref[...], high) + mm(btr_ref[...], low)
-        fl_own[h, 128:136, :] = jnp.broadcast_to(decay_of(h), (8, 128))
+        state = mm(btr_ref[...], high) + mm(btr_ref[...], low)
+        for k in range(2):
+            fl_own[h + k, 0:128, :] = state[:, k * 128 : k * 128 + 128]
+            fl_own[h + k, 128:136, :] = jnp.broadcast_to(decay_of(h + k), (8, 128))
 
     def to_sibling(source, target, sem):
         return pltpu.make_async_remote_copy(
@@ -243,7 +256,7 @@
         return to_sibling(own.at[pl.ds(theirs + part * pair, pair)], got.at[pl.ds(part * pair, pair)], sem)
 
     def heads_of(base, part, act):
-        loop(0, pair, lambda i: act(base + part * pair + i))
+        act(base + part * pair)
 
     def ring_start(source, target, part, rows_sent, sem):
         def start(other):
@@ -310,6 +323,8 @@
     skips_ref[...] = jnp.broadcast_to(as_column(skip_ref[...]), (heads, 128))
     ctr_ref[...] = c_ref[...].astype(F32).T.astype(BF16)
     scores_ref[...] = mm(c_ref[...], b_ref[...], NT)
+    cc_ref[...] = jnp.concatenate([c_ref[...], c_ref[...]], axis=1)
+    bb_ref[...] = jnp.concatenate([b_ref[...], b_ref[...]], axis=1)
 
     def near(h):
         cols = columns_of(h)
@@ -317,7 +332,11 @@
         weights = scores_ref[...] * jnp.exp(gap) * step_row(h)
         high, low = split2(weights)
         x_h = x_ref[:, channels(h)]
-        mixed_ref[:, channels(h)] = mm(high, x_h) + mm(low, x_h)
+        wide_x = x_h.astype(F32)
+        mixed_ref[:, channels(h)] = mm(high, x_h) + mm(low, x_h) + skip_of(h) * wide_x
+        u_ref[:, channels(h)] = gain_ref[:, channels(h)] * (wide_x - target_ref[:, channels(h)].astype(F32))
+        expb_ref[:, channels(h)] = jnp.broadcast_to(cols[EXPCUM], (tokens, 128))
+        endwb_ref[:, channels(h)] = jnp.broadcast_to(cols[ENDW], (tokens, 128))
 
     loop(0, heads, near)
     sum_ref[...] = jnp.zeros_like(sum_ref)
@@ -344,17 +363,21 @@
         here = pl.ds(part * pair, pair)
         return to_sibling(own.at[here], got.at[here], sem)
 
+    def stacked(ref, h):
+        high, low = split2(two(lambda k: ref[h + k]))
+        return jnp.concatenate([high, low], axis=0)
+
     def far(h):
-        cols = columns_of(h)
-        high, low = split2(sin_ref[h])
-        reached = mm(c_ref[...], high) + mm(c_ref[...], low)
-        x_h = x_ref[:, channels(h)].astype(F32)
-        mixed = mixed_ref[:, channels(h)] + cols[EXPCUM] * reached + skip_of(h) * x_h
-        mixed_ref[:, channels(h)] = mixed
-        gained = gain_ref[:, channels(h)] * mixed
-        sum_ref[0] += mixed * mixed
-        sum_ref[1] += gained * (x_h - target_ref[:, channels(h)].astype(F32))
-        sum_ref[2] += gained * gained
+        reached = mm(cc_ref[...], stacked(sin_ref, h))
+        sums = [0.0, 0.0, 0.0]
+        for k in range(2):
+            here = channels(h + k)
+            mixed = mixed_ref[:, here] + expb_ref[:, here] * reached[:, k * 128 : k * 128 + 128]
+            mixed_ref[:, here] = mixed
+            gained = gain_ref[:, here] * mixed
+            sums = [sums[0] + mixed * mixed, sums[1] + u_ref[:, here] * mixed, sums[2] + gained * gained]
+        for i in range(3):
+            sum_ref[i] += sums[i]
 
     for part in range(parts):
         ring_all(fp_out, fp_in, part, piece, 2 + part).wait_recv()
@@ -393,18 +416,24 @@
     inner = total[1:2, :] + inv_scale * total[2:3, :]
     coef = inner * inv_scale * inv_scale * inv_scale / width
     back = jnp.concatenate([inv_scale, coef, jnp.zeros((126, tokens), F32)], axis=0).T
-    inv_col, coef_col = back[:, 0:1], back[:, 1:2]
+    inv_col = jnp.broadcast_to(back[:, 0:1], (tokens, 128))
+    scale_ref[0] = inv_col
+    scale_ref[1] = inv_col * inv_col
+    scale_ref[2] = jnp.broadcast_to(back[:, 1:2], (tokens, 128))
 
     def norm_back(h):
-        gain = gain_ref[:, channels(h)]
-        mixed = mixed_ref[:, channels(h)]
-        x_h = x_ref[:, channels(h)].astype(F32)
-        grad_out = x_h + gain * mixed * inv_col - target_ref[:, channels(h)].astype(F32)
-        grad_mixed = gain * grad_out * inv_col - mixed * coef_col
-        gm_ref[:, channels(h)] = grad_mixed
-        gx_ref[:, channels(h)] = grad_out + skip_of(h) * grad_mixed
-        high, low = split2(grad_mixed * columns_of(h)[EXPCUM])
-        bl_own[h] = mm(ctr_ref[...], high) + mm(ctr_ref[...], low)
+        def weighted(k):
+            here = channels(h + k)
+            gain = gain_ref[:, here]
+            factor = (gain * gain) * scale_ref[1] - scale_ref[2]
+            grad_mixed = u_ref[:, here] * scale_ref[0] + mixed_ref[:, here] * factor
+            gm_ref[:, here] = grad_mixed
+            return grad_mixed * expb_ref[:, here]
+
+        high, low = split2(two(weighted))
+        state = mm(ctr_ref[...], high) + mm(ctr_ref[...], low)
+        for k in range(2):
+            bl_own[h + k] = state[:, k * 128 : k * 128 + 128]
 
     def join_back(part):
         for i in range(pair):
@@ -429,17 +458,23 @@
 
     def near_back(h):
         cols = columns_of(h)
+        here = channels(h)
         gap = jnp.where(along_iota >= down_iota, cum_row(h) - cols[CUM], -1e30)
         decay = jnp.exp(gap)
-        grad_mixed = gm_ref[:, channels(h)]
+        grad_mixed = gm_ref[:, here]
         gm_parts = split2(grad_mixed)
-        x_h = x_ref[:, channels(h)]
-        y_ref[:, channels(h)] = mm3(split2(scores_ref[...] * decay), gm_parts)
+        x_h = x_ref[:, here]
+        wide_x = x_h.astype(F32)
+        mixed = mixed_ref[:, here]
+        value = mm3(split2(scores_ref[...] * decay), gm_parts)
+        grad_out = wide_x + gain_ref[:, here] * mixed * scale_ref[0] - target_ref[:, here].astype(F32)
+        gx_ref[:, here] = grad_out + skip_of(h) * grad_mixed + cols[STEP] * value
         grad_weights = mm(x_h, gm_parts[0], NT) + mm(x_h, gm_parts[1], NT)
         dst_ref[...] += grad_weights * decay * cols[STEP]
-        own = grad_mixed * (mixed_ref[:, channels(h)] - skip_of(h) * x_h.astype(F32))
-        rq_ref[...] = jnp.where(lane == h, jnp.sum(own, axis=1, keepdims=True), rq_ref[...])
-        gc_ref[...] += mm3(split2(grad_mixed * cols[EXPCUM]), split2(sin_ref[h]), NT)
+        row_sum = jnp.sum(grad_mixed * (mixed - skip_of(h) * wide_x), axis=1, keepdims=True)
+        column_sum = jnp.sum(wide_x * value, axis=1, keepdims=True)
+        rq_ref[...] = jnp.where(lane == h, row_sum, jnp.where(lane == h + 8, column_sum, rq_ref[...]))
+        gc_ref[...] += mm3(split2(grad_mixed * expb_ref[:, here]), split2(sin_ref[h]), NT)
 
     loop(0, heads, near_back)
     grad_scores = dst_ref[...]
@@ -467,18 +502,24 @@
             bs_out[at] = jnp.where(core == 0, for_second, for_first)
 
     def far_back(h):
-        cols = columns_of(h)
-        grad_state = gout_ref[h]
-        high, low = split2(grad_state)
-        x_h = x_ref[:, channels(h)]
-        reached = mm(b_ref[...], high) + mm(b_ref[...], low)
-        value = y_ref[:, channels(h)] + cols[ENDDEC] * reached
-        gx_ref[:, channels(h)] += cols[STEP] * value
-        own = jnp.sum(x_h.astype(F32) * value, axis=1, keepdims=True)
-        rq_ref[...] = jnp.where(lane == h + 8, own, rq_ref[...])
-        gb_ref[...] += cols[ENDW] * (mm(x_h, high, NT) + mm(x_h, low, NT))
-        leaving = decay_of(h) * sin_ref[h] + fl_own[h, 0:128, :]
-        ext_ref[pl.ds(h, 1), :] = jnp.sum(grad_state * leaving, axis=0, keepdims=True)
+        both_parts = stacked(gout_ref, h)
+        reached = mm(bb_ref[...], both_parts)
+        table = rq_ref[...]
+        grad_b = gb_ref[...]
+        for k in range(2):
+            here = channels(h + k)
+            at = slice(k * 128, k * 128 + 128)
+            x_h = x_ref[:, here]
+            weight = endwb_ref[:, here]
+            gx_ref[:, here] += weight * reached[:, at]
+            row_sum = jnp.sum(x_h.astype(F32) * reached[:, at], axis=1, keepdims=True)
+            table = jnp.where(lane == h + k + 16, row_sum, table)
+            parts_along = jnp.concatenate([both_parts[0:128, at], both_parts[128:256, at]], axis=1)
+            grad_b = grad_b + weight * mm(jnp.concatenate([x_h, x_h], axis=1), parts_along, NT)
+            leaving = decay_of(h + k) * sin_ref[h + k] + fl_own[h + k, 0:128, :]
+            ext_ref[pl.ds(h + k, 1), :] = jnp.sum(gout_ref[h + k] * leaving, axis=0, keepdims=True)
+        rq_ref[...] = table
+        gb_ref[...] = grad_b
 
     for part in range(parts):
         ring_all(bp_out, bp_in, part, piece, 6 + part).wait_recv()
@@ -492,13 +533,11 @@
         heads_of(theirs, part, far_back)
 
     ends = rq_ref[...].T
-    inner_x = ends[8 : 8 + heads, :]
+    inner_x = ends[8 : 8 + heads, :] + rows_ref[2] * ends[16 : 16 + heads, :]
     extra = jnp.sum(ext_ref[...], axis=1, keepdims=True)
-    token_iota = lax.broadcasted_iota(jnp.int32, (heads, tokens), 1)
-    grad_cum = ends[0:heads, :] - step * inner_x + jnp.where(token_iota == tokens - 1, extra, 0.0)
     lower = (down_iota >= along_iota).astype(F32).astype(BF16)
-    high, mid, low = split3(grad_cum)
-    grad_dec = mm(high, lower) + (mm(mid, lower) + mm(low, lower))
+    high, mid, low = split3(ends[0:heads, :] - step * inner_x)
+    grad_dec = mm(high, lower) + (mm(mid, lower) + mm(low, lower)) + extra
     gs_ref[...] = inner_x - rate * grad_dec
 
     for part in range(parts):
@@ -561,7 +600,7 @@
         out_specs=[vmem] * 4,
         scratch_shapes=[buffer(*operand.shape, dtype=operand.dtype) for operand in operands]
         + [
-            buffer(2, heads, tokens),
+            buffer(3, heads, tokens),
             buffer(tokens, 128),
             buffer(heads, 128),
             buffer(heads, 128),
@@ -569,6 +608,11 @@
             buffer(tokens, wide),
             buffer(tokens, wide),
             buffer(tokens, wide),
+            buffer(tokens, wide),
+            buffer(tokens, wide),
+            buffer(tokens, 256, dtype=BF16),
+            buffer(tokens, 256, dtype=BF16),
+            buffer(3, tokens, 128),
             buffer(tokens, 128),
             buffer(heads, 128),
             buffer(*state),

time: 64.3 us -> 62.1 us (0.966)
  Pallas kernels: 63.5 us -> 61.3 us
    pallas_call x1, Pallas kernels: 62.5 us -> 60.2 us  [body(): pl.pallas_call(functools.partial(kernel, chips, ranks, float(wide * ranks...]
where the time goes in v4:
time: 62.1 us; the launch traced here: 62 us
  Pallas kernels  61.3 us (99%)
  between operations  0.64 us (1%)
    pallas_call x1, Pallas kernels, body(): pl.pallas_call(functools.partial(kernel, chips, ranks, float(wide * ranks...  60.2 us

profile of v4, /device:TPU:1, one launch (start us, length us, event | category | flops | bytes accessed | tf_op | source)
XLA Modules:
  0.0 62.0 jit_solution(2806891622922873653)
XLA Ops:
  0.6 60.2 %layer.1 = (f32[256,1024]{1,0:T(8,128)S(1)}, f32[256,128]{1,0:T(8,128)S(1)}, f32[256,128]{1,0:T(8,128)S(1)}, f32[8,256]{1,0:T(8,128)S(1)}) custom-call(bf16[256,1024]{1,0:T(8,128)(2,1)} %x_hbm.1, bf16[256,1024]{1,0:T(8,128)(2,1)} %target_hbm.1, bf16[256,128]{1,0:T(8,128)(2,1)} %bitcast.11, bf16[256,128]{1,0:T(8,128)(2,1)} %bitcast.12, f32[8,256]{1,0:T(8,128)} %bitcast.13, ...), custom_call_target="tpu_custom_call" | custom-call | tf_op jit(solution)/shard_map/layer/pallas_call | solution.py:596
  60.9 1.1 %copy_out.1 = (f32[256,1024]{1,0:T(8,128)}, f32[256,128]{1,0:T(8,128)}, f32[256,128]{1,0:T(8,128)}, f32[8,256]{1,0:T(8,128)}) custom-call(f32[256,1024]{1,0:T(8,128)S(1)} %get-tuple-element.12.refs_0_, f32[256,128]{1,0:T(8,128)S(1)} %get-tuple-element.13.refs_1_, f32[256,128]{1,0:T(8,128)S(1)} %get-tuple-element.14.refs_2_, ...), custom_call_target="tpu_custom_call" | custom-call | tf_op jit(solution)/shard_map/copy_out/pallas_call | solution.py:655

commit v5 on v4

--- a/solution.py
+++ b/solution.py
@@ -56,7 +56,9 @@
     gx_ref,
     gb_ref,
     gc_ref,
-    gs_ref,
+    rows_ref,
+    rq_ref,
+    ext_ref,
     x_ref,
     target_ref,
     b_ref,
@@ -66,7 +68,6 @@
     rate_ref,
     skip_ref,
     gain_ref,
-    rows_ref,
     cols_ref,
     ends_ref,
     skips_ref,
@@ -79,8 +80,6 @@
     cc_ref,
     bb_ref,
     scale_ref,
-    rq_ref,
-    ext_ref,
     sin_ref,
     gout_ref,
     btr_ref,
@@ -94,7 +93,6 @@
     fp_out,
     fp_in,
     fs_out,
-    fs_in,
     bl_own,
     bl_got,
     bm_out,
@@ -102,7 +100,6 @@
     bp_out,
     bp_in,
     bs_out,
-    bs_in,
     z_out,
     z_in,
     load_sem,
@@ -201,6 +198,7 @@
     rows_ref[0] = cum
     rows_ref[1] = step
     rows_ref[2] = enddec
+    rows_ref[3] = jnp.broadcast_to(rate, (heads, tokens))
     ends_ref[...] = jnp.broadcast_to(jnp.exp(last), (heads, 128))
     table = jnp.concatenate(table + [jnp.zeros((128 - heads * len(table), tokens), F32)], axis=0)
     cols_ref[...] = table.T
@@ -307,16 +305,17 @@
                 (decay0 * decay1)[None], (per_head, 8, 128)
             )
 
+    loop(0, half, lambda i: local_state(2 * i))
+    pl.semaphore_wait(barrier, (chips - 1) + (ranks - 1) + 1)
     for part in range(parts):
-        heads_of(theirs, part, local_state)
-        if part == 0:
-            pl.semaphore_wait(barrier, (chips - 1) + (ranks - 1) + 1)
         swap_of(fl_own, fl_got, part, part).start()
-    for part in range(parts):
-        heads_of(mine, part, local_state)
+
+    def first_round(part):
         swap_of(fl_own, fl_got, part, part).wait_recv()
         join_forward(part)
         ring_start(fm_out, fm_in, part, piece + 1, part)
+
+    loop(0, parts, first_round)
 
     for load in loads[5:]:
         load.wait()
@@ -341,13 +340,15 @@
     loop(0, heads, near)
     sum_ref[...] = jnp.zeros_like(sum_ref)
 
-    for part in range(parts):
+    def scan_forward(part):
         ring_all(fm_out, fm_in, part, piece + 1, part).wait_recv()
         state = jnp.zeros((piece, 128), F32)
         for t in range(chips):
             fp_out[part, t] = state
             state = fm_in[part, t, piece : piece + 1, :] * state + fm_in[part, t, 0:piece, :]
         ring_start(fp_out, fp_in, part, piece, 2 + part)
+
+    loop(0, parts, scan_forward)
 
     def enter(part):
         for i in range(pair):
@@ -360,8 +361,7 @@
             fs_out[at] = jnp.where(core == 0, for_second, for_first)
 
     def both(own, got, part, sem):
-        here = pl.ds(part * pair, pair)
-        return to_sibling(own.at[here], got.at[here], sem)
+        return to_sibling(own.at[pl.ds(part * pair, pair)], got.at[pl.ds(mine + part * pair, pair)], sem)
 
     def stacked(ref, h):
         high, low = split2(two(lambda k: ref[h + k]))
@@ -379,22 +379,26 @@
         for i in range(3):
             sum_ref[i] += sums[i]
 
-    for part in range(parts):
+    def far_mine(part):
         ring_all(fp_out, fp_in, part, piece, 2 + part).wait_recv()
         enter(part)
-        both(fs_out, fs_in, part, 2 + part).start()
+        both(fs_out, sin_ref, part, 2 + part).start()
         heads_of(mine, part, far)
-    for part in range(parts):
-        both(fs_out, fs_in, part, 2 + part).wait_recv()
-        for i in range(pair):
-            sin_ref[theirs + part * pair + i] = fs_in[part * pair + i]
+
+    def far_theirs(part):
+        both(fs_out, sin_ref, part, 2 + part).wait_recv()
         heads_of(theirs, part, far)
 
+    loop(0, parts, far_mine)
+    loop(0, parts, far_theirs)
+
     lane = lax.broadcasted_iota(jnp.int32, (tokens, 128), 1)
-    packed = jnp.zeros((tokens, 128), F32)
+    row_iota = lax.broadcasted_iota(jnp.int32, (8, 256), 0)
+    sums = jnp.zeros((8, tokens), F32)
     for i in range(3):
-        packed = jnp.where(lane == i, jnp.sum(sum_ref[i], axis=1, keepdims=True), packed)
-    z_out[...] = packed.T[0:8, :]
+        ones = (row_iota == i).astype(F32).astype(BF16)
+        sums = sums + mm(ones, jnp.concatenate(split2(sum_ref[i]), axis=1), NT)
+    z_out[...] = sums
 
     def z_copy(to, slot):
         return pltpu.make_async_remote_copy(
@@ -441,14 +445,18 @@
             decay0, _ = decay_pair(part * pair + i)
             bm_out[owners_of(part, i)] = (decay0 * second + first).reshape(per_head, piece, 128)
 
-    for part in range(parts):
+    def back_theirs(part):
         heads_of(theirs, part, norm_back)
         swap_of(bl_own, bl_got, part, 4 + part).start()
-    for part in range(parts):
+
+    def back_mine(part):
         heads_of(mine, part, norm_back)
         swap_of(bl_own, bl_got, part, 4 + part).wait_recv()
         join_back(part)
         ring_start(bm_out, bm_in, part, piece, 4 + part)
+
+    loop(0, parts, back_theirs)
+    loop(0, parts, back_mine)
 
     rq_ref[...] = jnp.zeros_like(rq_ref)
     gc_ref[...] = jnp.zeros_like(gc_ref)
@@ -483,13 +491,15 @@
     high, low = split2(grad_scores.T)
     gc_ref[...] += mm(high, b_ref[...]) + mm(low, b_ref[...])
 
-    for part in range(parts):
+    def scan_back(part):
         ring_all(bm_out, bm_in, part, piece, 4 + part).wait_recv()
         grad = jnp.zeros((piece, 128), F32)
         for t in reversed(range(chips)):
             bp_out[part, t] = grad
             grad = fm_in[part, t, piece : piece + 1, :] * grad + bm_in[part, t]
         ring_start(bp_out, bp_in, part, piece, 6 + part)
+
+    loop(0, parts, scan_back)
 
     def leave(part):
         for i in range(pair):
@@ -521,30 +531,24 @@
         rq_ref[...] = table
         gb_ref[...] = grad_b
 
-    for part in range(parts):
+    def last_mine(part):
         ring_all(bp_out, bp_in, part, piece, 6 + part).wait_recv()
         leave(part)
-        both(bs_out, bs_in, part, 6 + part).start()
+        both(bs_out, gout_ref, part, 6 + part).start()
         heads_of(mine, part, far_back)
-    for part in range(parts):
-        both(bs_out, bs_in, part, 6 + part).wait_recv()
-        for i in range(pair):
-            gout_ref[theirs + part * pair + i] = bs_in[part * pair + i]
+
+    def last_theirs(part):
+        both(bs_out, gout_ref, part, 6 + part).wait_recv()
         heads_of(theirs, part, far_back)
 
-    ends = rq_ref[...].T
-    inner_x = ends[8 : 8 + heads, :] + rows_ref[2] * ends[16 : 16 + heads, :]
-    extra = jnp.sum(ext_ref[...], axis=1, keepdims=True)
-    lower = (down_iota >= along_iota).astype(F32).astype(BF16)
-    high, mid, low = split3(ends[0:heads, :] - step * inner_x)
-    grad_dec = mm(high, lower) + (mm(mid, lower) + mm(low, lower)) + extra
-    gs_ref[...] = inner_x - rate * grad_dec
+    loop(0, parts, last_mine)
+    loop(0, parts, last_theirs)
 
     for part in range(parts):
         swap_of(fl_own, fl_got, part, part).wait_send()
-        both(fs_out, fs_in, part, 2 + part).wait_send()
+        both(fs_out, sin_ref, part, 2 + part).wait_send()
         swap_of(bl_own, bl_got, part, 4 + part).wait_send()
-        both(bs_out, bs_in, part, 6 + part).wait_send()
+        both(bs_out, gout_ref, part, 6 + part).wait_send()
         ring_all(fm_out, fm_in, part, piece + 1, part).wait_send()
         ring_all(fp_out, fp_in, part, piece, 2 + part).wait_send()
         ring_all(bm_out, bm_in, part, piece, 4 + part).wait_send()
@@ -552,14 +556,27 @@
     other_ranks(lambda other: z_copy(other, other).wait_send())
 
 
-def copy_out(*refs):
-    count = len(refs) // 2
-    sources, targets, sems = refs[:count], refs[count:-1], refs[-1]
-    copies = [pltpu.make_async_copy(s, t, sems.at[i]) for i, (s, t) in enumerate(zip(sources, targets))]
+def finish(gx_in, gb_in, gc_in, rows_ref, rq_ref, ext_ref, gx_ref, gb_ref, gc_ref, gs_ref, sums_ref, sems):
+    pairs = ((gx_in, gx_ref), (gb_in, gb_ref), (gc_in, gc_ref))
+    copies = [pltpu.make_async_copy(source, target, sems.at[i]) for i, (source, target) in enumerate(pairs)]
     for copy in copies:
         copy.start()
+    heads, tokens = sums_ref.shape
+    step, enddec, rate = rows_ref[1], rows_ref[2], rows_ref[3]
+    ends = rq_ref[...].T
+    inner_x = ends[8 : 8 + heads, :] + enddec * ends[16 : 16 + heads, :]
+    extra = jnp.sum(ext_ref[...], axis=1, keepdims=True)
+    down_iota = lax.broadcasted_iota(jnp.int32, (tokens, tokens), 0)
+    along_iota = lax.broadcasted_iota(jnp.int32, (tokens, tokens), 1)
+    lower = (down_iota >= along_iota).astype(F32).astype(BF16)
+    high, mid, low = split3(ends[0:heads, :] - step * inner_x)
+    grad_dec = mm(high, lower) + (mm(mid, lower) + mm(low, lower)) + extra
+    sums_ref[...] = inner_x - rate * grad_dec
+    last = pltpu.make_async_copy(sums_ref, gs_ref, sems.at[3])
+    last.start()
     for copy in copies:
         copy.wait()
+    last.wait()
 
 
 def body(chips, ranks, inputs, b_proj, c_proj, step_sizes, log_rate, forget, skip_gain, norm_gain, target):
@@ -595,12 +612,16 @@
     )
     results = pl.pallas_call(
         functools.partial(kernel, chips, ranks, float(wide * ranks)),
-        out_shape=out_shape,
+        out_shape=out_shape[0:3]
+        + (
+            jax.ShapeDtypeStruct((4, heads, tokens), F32),
+            jax.ShapeDtypeStruct((tokens, 128), F32),
+            jax.ShapeDtypeStruct((heads, 128), F32),
+        ),
         in_specs=[hbm] * len(operands),
-        out_specs=[vmem] * 4,
+        out_specs=[vmem] * 6,
         scratch_shapes=[buffer(*operand.shape, dtype=operand.dtype) for operand in operands]
         + [
-            buffer(3, heads, tokens),
             buffer(tokens, 128),
             buffer(heads, 128),
             buffer(heads, 128),
@@ -613,8 +634,6 @@
             buffer(tokens, 256, dtype=BF16),
             buffer(tokens, 256, dtype=BF16),
             buffer(3, tokens, 128),
-            buffer(tokens, 128),
-            buffer(heads, 128),
             buffer(*state),
             buffer(*state),
             buffer(128, tokens, dtype=BF16),
@@ -628,14 +647,12 @@
             buffer(2, chips, piece, 128),
             buffer(2, chips, piece, 128),
             buffer(*half_state),
-            buffer(*half_state),
             buffer(*state),
             buffer(*half_state),
             buffer(2, chips, piece, 128),
             buffer(2, chips, piece, 128),
             buffer(2, chips, piece, 128),
             buffer(2, chips, piece, 128),
-            buffer(*half_state),
             buffer(*half_state),
             buffer(8, tokens),
             buffer(ranks, 8, tokens),
@@ -653,13 +670,13 @@
         name="layer",
     )(*operands)
     grad_x, grad_b, grad_c, grad_steps = pl.pallas_call(
-        copy_out,
+        finish,
         out_shape=out_shape,
-        in_specs=[pl.BlockSpec(memory_space=pl.ANY)] * 4,
+        in_specs=[pl.BlockSpec(memory_space=pl.ANY)] * 3 + [vmem] * 3,
         out_specs=[hbm] * 4,
-        scratch_shapes=[pltpu.SemaphoreType.DMA((4,))],
-        compiler_params=pltpu.CompilerParams(vmem_limit_bytes=1024 * 1024),
-        name="copy_out",
+        scratch_shapes=[buffer(heads, tokens), pltpu.SemaphoreType.DMA((4,))],
+        compiler_params=pltpu.CompilerParams(vmem_limit_bytes=4 * 1024 * 1024),
+        name="finish",
     )(*results)
     return (
         grad_x,

time: 62.1 us -> 62.4 us (level)
  no operation moved by 1% of the time
where the time goes in v5:
time: 62.4 us; the launch traced here: 62.3 us
  Pallas kernels  61.6 us (99%)
  between operations  0.64 us (1%)
    pallas_call x1, Pallas kernels, body(): pl.pallas_call(functools.partial(kernel, chips, ranks, float(wide * ranks...  60.5 us

profile of v5, /device:TPU:1, one launch (start us, length us, event | category | flops | bytes accessed | tf_op | source)
XLA Modules:
  0.0 62.3 jit_solution(1432021183816243650)
XLA Ops:
  0.6 60.5 %layer.1 = (f32[256,1024]{1,0:T(8,128)S(1)}, f32[256,128]{1,0:T(8,128)S(1)}, f32[256,128]{1,0:T(8,128)S(1)}, f32[4,8,256]{2,1,0:T(8,128)S(1)}, f32[256,128]{1,0:T(8,128)S(1)}, /*index=5*/f32[8,128]{1,0:T(8,128)S(1)}) custom-call(bf16[256,1024]{1,0:T(8,128)(2,1)} %x_hbm.1, bf16[256,1024]{1,0:T(8,128)(2,1)} %target_hbm.1, bf16[256,128]{1,0:T(8,128)(2,1)} %bitcast.11, ...), custom_call_target="tpu_custom_call" | custom-call | tf_op jit(solution)/shard_map/layer/pallas_call | solution.py:613
  61.2 1.1 %finish.1 = (f32[256,1024]{1,0:T(8,128)}, f32[256,128]{1,0:T(8,128)}, f32[256,128]{1,0:T(8,128)}, f32[8,256]{1,0:T(8,128)}) custom-call(f32[256,1024]{1,0:T(8,128)S(1)} %get-tuple-element.14.gx_in, f32[256,128]{1,0:T(8,128)S(1)} %get-tuple-element.15.gb_in, f32[256,128]{1,0:T(8,128)S(1)} %get-tuple-element.16.gc_in, ...), custom_call_target="tpu_custom_call" | custom-call | tf_op jit(solution)/shard_map/finish/pallas_call | solution.py:672

commit v6 on v5

--- a/solution.py
+++ b/solution.py
@@ -73,7 +73,6 @@
     skips_ref,
     scores_ref,
     mixed_ref,
-    gm_ref,
     u_ref,
     expb_ref,
     endwb_ref,
@@ -93,8 +92,13 @@
     fp_out,
     fp_in,
     fs_out,
-    bl_own,
-    bl_got,
+    bl_second,
+    su_ref,
+    sm_ref,
+    se_ref,
+    sc_ref,
+    cf_ref,
+    sct_ref,
     bm_out,
     bm_in,
     bp_out,
@@ -120,7 +124,8 @@
     ctx = lax.axis_index("ctx")
     rank = lax.axis_index("head")
     chip, core = lax.div(ctx, 2), lax.rem(ctx, 2)
-    sibling = (chip * 2 + 1 - core, rank)
+    twin = chip * 2 + 1 - core
+    sibling = (twin, rank)
     lines = chips // 4
     line, place = lax.div(chip, 4), lax.rem(chip, 4)
 
@@ -131,18 +136,14 @@
 
         lax.fori_loop(low, high, turn, 0)
 
+    lines_from = [lax.rem(line + down, lines) * 4 for down in range(lines)]
+    columns_from = [lax.rem(place + along, 4) for along in range(4)]
+    offsets = [(down, along) for down in range(lines) for along in range(4)][1:]
+    offsets.sort(key=lambda o: -(min(o[0], lines - o[0]) + min(o[1], 4 - o[1])))
+
     def other_chips(act):
-        columns = [lax.rem(place + along, 4) for along in (2, 1, 3, 0)]
-
-        def on_line(q, count):
-            down = lines // 2 + (1 - 2 * lax.rem(q, 2)) * lax.div(q + 1, 2)
-            base = lax.rem(line + down, lines) * 4
-            for column in columns[:count]:
-                act(base + column)
-
-        if lines > 1:
-            loop(0, lines - 1, lambda q: on_line(q, 4))
-        on_line(jnp.int32(lines - 1), 3)
+        for down, along in offsets:
+            act(lines_from[down] + columns_from[along])
 
     def other_ranks(act):
         for away in sorted(range(1, ranks), key=lambda k: -min(k, ranks - k)):
@@ -155,6 +156,7 @@
 
     other_chips(lambda other: greet((other * 2 + core, rank)))
     other_ranks(lambda other: greet((ctx, other)))
+    other_ranks(lambda other: greet((twin, other)))
     greet(sibling)
 
     loads = [
@@ -306,7 +308,7 @@
             )
 
     loop(0, half, lambda i: local_state(2 * i))
-    pl.semaphore_wait(barrier, (chips - 1) + (ranks - 1) + 1)
+    pl.semaphore_wait(barrier, (chips - 1) + 2 * (ranks - 1) + 1)
     for part in range(parts):
         swap_of(fl_own, fl_got, part, part).start()
 
@@ -320,7 +322,8 @@
     for load in loads[5:]:
         load.wait()
     skips_ref[...] = jnp.broadcast_to(as_column(skip_ref[...]), (heads, 128))
-    ctr_ref[...] = c_ref[...].astype(F32).T.astype(BF16)
+    cf_ref[...] = c_ref[...].astype(F32).T
+    ctr_ref[...] = cf_ref[...].astype(BF16)
     scores_ref[...] = mm(c_ref[...], b_ref[...], NT)
     cc_ref[...] = jnp.concatenate([c_ref[...], c_ref[...]], axis=1)
     bb_ref[...] = jnp.concatenate([b_ref[...], b_ref[...]], axis=1)
@@ -338,6 +341,23 @@
         endwb_ref[:, channels(h)] = jnp.broadcast_to(cols[ENDW], (tokens, 128))
 
     loop(0, heads, near)
+
+    def channels_of(base, count):
+        return pl.ds(pl.multiple_of(base * chan, chan), count * chan)
+
+    def to_twin():
+        return (
+            to_sibling(u_ref.at[:, channels_of(theirs, half)], su_ref, 8),
+            to_sibling(expb_ref.at[:, channels_of(theirs, half)], se_ref, 9),
+            to_sibling(cf_ref, sc_ref, 10),
+        )
+
+    def mixed_to_twin(part):
+        source = mixed_ref.at[:, channels_of(theirs + part * pair, pair)]
+        return to_sibling(source, sm_ref.at[:, channels_of(part * pair, pair)], 4 + part)
+
+    for copy in to_twin():
+        copy.start()
     sum_ref[...] = jnp.zeros_like(sum_ref)
 
     def scan_forward(part):
@@ -388,6 +408,7 @@
     def far_theirs(part):
         both(fs_out, sin_ref, part, 2 + part).wait_recv()
         heads_of(theirs, part, far)
+        mixed_to_twin(part).start()
 
     loop(0, parts, far_mine)
     loop(0, parts, far_theirs)
@@ -400,63 +421,72 @@
         sums = sums + mm(ones, jnp.concatenate(split2(sum_ref[i]), axis=1), NT)
     z_out[...] = sums
 
-    def z_copy(to, slot):
+    def z_copy(block, to, slot):
         return pltpu.make_async_remote_copy(
             src_ref=z_out,
-            dst_ref=z_in.at[slot],
-            send_sem=z_send.at[to],
-            recv_sem=z_recv.at[slot],
-            device_id=(ctx, to),
+            dst_ref=z_in.at[block, slot],
+            send_sem=z_send.at[block, to],
+            recv_sem=z_recv.at[block, slot],
+            device_id=(twin if block else ctx, to),
             device_id_type=MESH,
         )
 
-    other_ranks(lambda other: z_copy(other, rank).start())
-    z_in[rank] = z_out[...]
-    other_ranks(lambda other: z_copy(other, other).wait_recv())
-    total = z_in[0]
-    for i in range(1, ranks):
-        total = total + z_in[i]
-    inv_scale = lax.rsqrt(total[0:1, :] / width + EPSILON)
-    inner = total[1:2, :] + inv_scale * total[2:3, :]
-    coef = inner * inv_scale * inv_scale * inv_scale / width
-    back = jnp.concatenate([inv_scale, coef, jnp.zeros((126, tokens), F32)], axis=0).T
-    inv_col = jnp.broadcast_to(back[:, 0:1], (tokens, 128))
-    scale_ref[0] = inv_col
-    scale_ref[1] = inv_col * inv_col
-    scale_ref[2] = jnp.broadcast_to(back[:, 1:2], (tokens, 128))
-
-    def norm_back(h):
-        def weighted(k):
-            here = channels(h + k)
-            gain = gain_ref[:, here]
-            factor = (gain * gain) * scale_ref[1] - scale_ref[2]
-            grad_mixed = u_ref[:, here] * scale_ref[0] + mixed_ref[:, here] * factor
-            gm_ref[:, here] = grad_mixed
+    other_ranks(lambda other: z_copy(0, other, rank).start())
+    other_ranks(lambda other: z_copy(1, other, rank).start())
+    z_copy(1, rank, rank).start()
+    z_in[0, rank] = z_out[...]
+    for copy in to_twin():
+        copy.wait_recv()
+    sct_ref[...] = sc_ref[...].astype(BF16)
+    z_copy(1, rank, rank).wait_recv()
+    other_ranks(lambda other: z_copy(0, other, other).wait_recv())
+    other_ranks(lambda other: z_copy(1, other, other).wait_recv())
+    factors = []
+    for block in range(2):
+        total = z_in[block, 0]
+        for i in range(1, ranks):
+            total = total + z_in[block, i]
+        inv_scale = lax.rsqrt(total[0:1, :] / width + EPSILON)
+        inner = total[1:2, :] + inv_scale * total[2:3, :]
+        factors += [inv_scale, inner * inv_scale * inv_scale * inv_scale / width]
+    back = jnp.concatenate(factors + [jnp.zeros((124, tokens), F32)], axis=0).T
+    for block in range(2):
+        inv_col = jnp.broadcast_to(back[:, 2 * block : 2 * block + 1], (tokens, 128))
+        scale_ref[3 * block] = inv_col
+        scale_ref[3 * block + 1] = inv_col * inv_col
+        scale_ref[3 * block + 2] = jnp.broadcast_to(back[:, 2 * block + 1 : 2 * block + 2], (tokens, 128))
+
+    def norm_grad(gained, mixed, gain, block):
+        factor = (gain * gain) * scale_ref[3 * block + 1] - scale_ref[3 * block + 2]
+        return gained * scale_ref[3 * block] + mixed * factor
+
+    def back_round(part):
+        mixed_to_twin(part).wait_recv()
+
+        def own(k):
+            here = channels(mine + part * pair + k)
+            grad_mixed = norm_grad(u_ref[:, here], mixed_ref[:, here], gain_ref[:, here], 0)
             return grad_mixed * expb_ref[:, here]
 
-        high, low = split2(two(weighted))
-        state = mm(ctr_ref[...], high) + mm(ctr_ref[...], low)
-        for k in range(2):
-            bl_own[h + k] = state[:, k * 128 : k * 128 + 128]
-
-    def join_back(part):
+        def others(k):
+            at = channels(part * pair + k)
+            gain = gain_ref[:, channels(mine + part * pair + k)]
+            return norm_grad(su_ref[:, at], sm_ref[:, at], gain, 1) * se_ref[:, at]
+
+        high, low = split2(two(own))
+        own_state = mm(ctr_ref[...], high) + mm(ctr_ref[...], low)
+        high, low = split2(two(others))
+        got_state = mm(sct_ref[...], high) + mm(sct_ref[...], low)
+        first = jnp.where(core == 0, own_state, got_state)
+        second = jnp.where(core == 0, got_state, own_state)
         for i in range(pair):
-            first, second = pair_of(bl_own, bl_got, part * pair + i)
+            at = slice(i * 128, i * 128 + 128)
             decay0, _ = decay_pair(part * pair + i)
-            bm_out[owners_of(part, i)] = (decay0 * second + first).reshape(per_head, piece, 128)
-
-    def back_theirs(part):
-        heads_of(theirs, part, norm_back)
-        swap_of(bl_own, bl_got, part, 4 + part).start()
-
-    def back_mine(part):
-        heads_of(mine, part, norm_back)
-        swap_of(bl_own, bl_got, part, 4 + part).wait_recv()
-        join_back(part)
+            bl_second[part * pair + i] = second[:, at]
+            bm_out[owners_of(part, i)] = (decay0 * second[:, at] + first[:, at]).reshape(per_head, piece, 128)
         ring_start(bm_out, bm_in, part, piece, 4 + part)
 
-    loop(0, parts, back_theirs)
-    loop(0, parts, back_mine)
+    loop(0, parts, back_round)
 
     rq_ref[...] = jnp.zeros_like(rq_ref)
     gc_ref[...] = jnp.zeros_like(gc_ref)
@@ -469,11 +499,11 @@
         here = channels(h)
         gap = jnp.where(along_iota >= down_iota, cum_row(h) - cols[CUM], -1e30)
         decay = jnp.exp(gap)
-        grad_mixed = gm_ref[:, here]
+        mixed = mixed_ref[:, here]
+        grad_mixed = norm_grad(u_ref[:, here], mixed, gain_ref[:, here], 0)
         gm_parts = split2(grad_mixed)
         x_h = x_ref[:, here]
         wide_x = x_h.astype(F32)
-        mixed = mixed_ref[:, here]
         value = mm3(split2(scores_ref[...] * decay), gm_parts)
         grad_out = wide_x + gain_ref[:, here] * mixed * scale_ref[0] - target_ref[:, here].astype(F32)
         gx_ref[:, here] = grad_out + skip_of(h) * grad_mixed + cols[STEP] * value
@@ -504,7 +534,7 @@
     def leave(part):
         for i in range(pair):
             at = part * pair + i
-            _, second = pair_of(bl_own, bl_got, at)
+            second = bl_second[at]
             _, decay1 = decay_pair(at)
             for_second = bp_in[owners_of(part, i)].reshape(128, 128)
             for_first = decay1 * for_second + second
@@ -547,13 +577,17 @@
     for part in range(parts):
         swap_of(fl_own, fl_got, part, part).wait_send()
         both(fs_out, sin_ref, part, 2 + part).wait_send()
-        swap_of(bl_own, bl_got, part, 4 + part).wait_send()
+        mixed_to_twin(part).wait_send()
         both(bs_out, gout_ref, part, 6 + part).wait_send()
         ring_all(fm_out, fm_in, part, piece + 1, part).wait_send()
         ring_all(fp_out, fp_in, part, piece, 2 + part).wait_send()
         ring_all(bm_out, bm_in, part, piece, 4 + part).wait_send()
         ring_all(bp_out, bp_in, part, piece, 6 + part).wait_send()
-    other_ranks(lambda other: z_copy(other, other).wait_send())
+    for copy in to_twin():
+        copy.wait_send()
+    other_ranks(lambda other: z_copy(0, other, other).wait_send())
+    other_ranks(lambda other: z_copy(1, other, other).wait_send())
+    z_copy(1, rank, rank).wait_send()
 
 
 def finish(gx_in, gb_in, gc_in, rows_ref, rq_ref, ext_ref, gx_ref, gb_ref, gc_ref, gs_ref, sums_ref, sems):
@@ -630,10 +664,9 @@
             buffer(tokens, wide),
             buffer(tokens, wide),
             buffer(tokens, wide),
-            buffer(tokens, wide),
             buffer(tokens, 256, dtype=BF16),
             buffer(tokens, 256, dtype=BF16),
-            buffer(3, tokens, 128),
+            buffer(6, tokens, 128),
             buffer(*state),
             buffer(*state),
             buffer(128, tokens, dtype=BF16),
@@ -647,22 +680,27 @@
             buffer(2, chips, piece, 128),
             buffer(2, chips, piece, 128),
             buffer(*half_state),
-            buffer(*state),
             buffer(*half_state),
+            buffer(tokens, wide // 2),
+            buffer(tokens, wide // 2),
+            buffer(tokens, wide // 2),
+            buffer(128, tokens),
+            buffer(128, tokens),
+            buffer(128, tokens, dtype=BF16),
             buffer(2, chips, piece, 128),
             buffer(2, chips, piece, 128),
             buffer(2, chips, piece, 128),
             buffer(2, chips, piece, 128),
             buffer(*half_state),
             buffer(8, tokens),
-            buffer(ranks, 8, tokens),
+            buffer(2, ranks, 8, tokens),
             pltpu.SemaphoreType.DMA((9,)),
+            pltpu.SemaphoreType.DMA((11,)),
+            pltpu.SemaphoreType.DMA((11,)),
             pltpu.SemaphoreType.DMA((8,)),
             pltpu.SemaphoreType.DMA((8,)),
-            pltpu.SemaphoreType.DMA((8,)),
-            pltpu.SemaphoreType.DMA((8,)),
-            pltpu.SemaphoreType.DMA((ranks,)),
-            pltpu.SemaphoreType.DMA((ranks,)),
+            pltpu.SemaphoreType.DMA((2, ranks)),
+            pltpu.SemaphoreType.DMA((2, ranks)),
         ],
         compiler_params=pltpu.CompilerParams(
             collective_id=0, has_side_effects=True, vmem_limit_bytes=24 * 1024 * 1024

time: 62.4 us -> 62.5 us (level)
  no operation moved by 1% of the time
where the time goes in v6:
time: 62.5 us; the launch traced here: 62.3 us
  Pallas kernels  61.7 us (99%)
  between operations  0.64 us (1%)
    pallas_call x1, Pallas kernels, body(): pl.pallas_call(functools.partial(kernel, chips, ranks, float(wide * ranks...  60.6 us

profile of v6, /device:TPU:1, one launch (start us, length us, event | category | flops | bytes accessed | tf_op | source)
XLA Modules:
  0.0 62.3 jit_solution(8566403039323232656)
XLA Ops:
  0.6 60.6 %layer.1 = (f32[256,1024]{1,0:T(8,128)S(1)}, f32[256,128]{1,0:T(8,128)S(1)}, f32[256,128]{1,0:T(8,128)S(1)}, f32[4,8,256]{2,1,0:T(8,128)S(1)}, f32[256,128]{1,0:T(8,128)S(1)}, /*index=5*/f32[8,128]{1,0:T(8,128)S(1)}) custom-call(bf16[256,1024]{1,0:T(8,128)(2,1)} %x_hbm.1, bf16[256,1024]{1,0:T(8,128)(2,1)} %target_hbm.1, bf16[256,128]{1,0:T(8,128)(2,1)} %bitcast.11, ...), custom_call_target="tpu_custom_call" | custom-call | tf_op jit(solution)/shard_map/layer/pallas_call | solution.py:647
  61.2 1.1 %finish.1 = (f32[256,1024]{1,0:T(8,128)}, f32[256,128]{1,0:T(8,128)}, f32[256,128]{1,0:T(8,128)}, f32[8,256]{1,0:T(8,128)}) custom-call(f32[256,1024]{1,0:T(8,128)S(1)} %get-tuple-element.14.gx_in, f32[256,128]{1,0:T(8,128)S(1)} %get-tuple-element.15.gb_in, f32[256,128]{1,0:T(8,128)S(1)} %get-tuple-element.16.gc_in, ...), custom_call_target="tpu_custom_call" | custom-call | tf_op jit(solution)/shard_map/finish/pallas_call | solution.py:710

commit v7 on v6

--- a/solution.py
+++ b/solution.py
@@ -408,7 +408,6 @@
     def far_theirs(part):
         both(fs_out, sin_ref, part, 2 + part).wait_recv()
         heads_of(theirs, part, far)
-        mixed_to_twin(part).start()
 
     loop(0, parts, far_mine)
     loop(0, parts, far_theirs)
@@ -434,6 +433,8 @@
     other_ranks(lambda other: z_copy(0, other, rank).start())
     other_ranks(lambda other: z_copy(1, other, rank).start())
     z_copy(1, rank, rank).start()
+    for part in range(parts):
+        mixed_to_twin(part).start()
     z_in[0, rank] = z_out[...]
     for copy in to_twin():
         copy.wait_recv()

time: 62.5 us -> 62.5 us (level)
  no operation moved by 1% of the time
where the time goes in v7:
time: 62.5 us; the launch traced here: 62.3 us
  Pallas kernels  61.7 us (99%)
  between operations  0.64 us (1%)
    pallas_call x1, Pallas kernels, body(): pl.pallas_call(functools.partial(kernel, chips, ranks, float(wide * ranks...  60.6 us

profile of v7, /device:TPU:1, one launch (start us, length us, event | category | flops | bytes accessed | tf_op | source)
XLA Modules:
  0.0 62.3 jit_solution(289539587145799716)
XLA Ops:
  0.6 60.6 %layer.1 = (f32[256,1024]{1,0:T(8,128)S(1)}, f32[256,128]{1,0:T(8,128)S(1)}, f32[256,128]{1,0:T(8,128)S(1)}, f32[4,8,256]{2,1,0:T(8,128)S(1)}, f32[256,128]{1,0:T(8,128)S(1)}, /*index=5*/f32[8,128]{1,0:T(8,128)S(1)}) custom-call(bf16[256,1024]{1,0:T(8,128)(2,1)} %x_hbm.1, bf16[256,1024]{1,0:T(8,128)(2,1)} %target_hbm.1, bf16[256,128]{1,0:T(8,128)(2,1)} %bitcast.11, ...), custom_call_target="tpu_custom_call" | custom-call | tf_op jit(solution)/shard_map/layer/pallas_call | solution.py:648
  61.3 1.1 %finish.1 = (f32[256,1024]{1,0:T(8,128)}, f32[256,128]{1,0:T(8,128)}, f32[256,128]{1,0:T(8,128)}, f32[8,256]{1,0:T(8,128)}) custom-call(f32[256,1024]{1,0:T(8,128)S(1)} %get-tuple-element.14.gx_in, f32[256,128]{1,0:T(8,128)S(1)} %get-tuple-element.15.gb_in, f32[256,128]{1,0:T(8,128)S(1)} %get-tuple-element.16.gc_in, ...), custom_call_target="tpu_custom_call" | custom-call | tf_op jit(solution)/shard_map/finish/pallas_call | solution.py:711

commit v8 on v5

--- a/solution.py
+++ b/solution.py
@@ -131,18 +131,18 @@
 
         lax.fori_loop(low, high, turn, 0)
 
+    lines_from = [lax.rem(line + down, lines) * 4 for down in range(lines)]
+    columns_from = [lax.rem(place + along, 4) for along in range(4)]
+    offsets = [(down, along) for down in range(lines) for along in range(4)][1:]
+    offsets.sort(key=lambda o: -(min(o[0], lines - o[0]) + min(o[1], 4 - o[1])))
+
+    def unrolled(count, act):
+        for i in range(count):
+            act(i)
+
     def other_chips(act):
-        columns = [lax.rem(place + along, 4) for along in (2, 1, 3, 0)]
-
-        def on_line(q, count):
-            down = lines // 2 + (1 - 2 * lax.rem(q, 2)) * lax.div(q + 1, 2)
-            base = lax.rem(line + down, lines) * 4
-            for column in columns[:count]:
-                act(base + column)
-
-        if lines > 1:
-            loop(0, lines - 1, lambda q: on_line(q, 4))
-        on_line(jnp.int32(lines - 1), 3)
+        for down, along in offsets:
+            act(lines_from[down] + columns_from[along])
 
     def other_ranks(act):
         for away in sorted(range(1, ranks), key=lambda k: -min(k, ranks - k)):
@@ -315,7 +315,7 @@
         join_forward(part)
         ring_start(fm_out, fm_in, part, piece + 1, part)
 
-    loop(0, parts, first_round)
+    unrolled(parts, first_round)
 
     for load in loads[5:]:
         load.wait()
@@ -348,7 +348,7 @@
             state = fm_in[part, t, piece : piece + 1, :] * state + fm_in[part, t, 0:piece, :]
         ring_start(fp_out, fp_in, part, piece, 2 + part)
 
-    loop(0, parts, scan_forward)
+    unrolled(parts, scan_forward)
 
     def enter(part):
         for i in range(pair):
@@ -389,8 +389,8 @@
         both(fs_out, sin_ref, part, 2 + part).wait_recv()
         heads_of(theirs, part, far)
 
-    loop(0, parts, far_mine)
-    loop(0, parts, far_theirs)
+    unrolled(parts, far_mine)
+    unrolled(parts, far_theirs)
 
     lane = lax.broadcasted_iota(jnp.int32, (tokens, 128), 1)
     row_iota = lax.broadcasted_iota(jnp.int32, (8, 256), 0)
@@ -455,8 +455,8 @@
         join_back(part)
         ring_start(bm_out, bm_in, part, piece, 4 + part)
 
-    loop(0, parts, back_theirs)
-    loop(0, parts, back_mine)
+    unrolled(parts, back_theirs)
+    unrolled(parts, back_mine)
 
     rq_ref[...] = jnp.zeros_like(rq_ref)
     gc_ref[...] = jnp.zeros_like(gc_ref)
@@ -499,7 +499,7 @@
             grad = fm_in[part, t, piece : piece + 1, :] * grad + bm_in[part, t]
         ring_start(bp_out, bp_in, part, piece, 6 + part)
 
-    loop(0, parts, scan_back)
+    unrolled(parts, scan_back)
 
     def leave(part):
         for i in range(pair):
@@ -541,8 +541,8 @@
         both(bs_out, gout_ref, part, 6 + part).wait_recv()
         heads_of(theirs, part, far_back)
 
-    loop(0, parts, last_mine)
-    loop(0, parts, last_theirs)
+    unrolled(parts, last_mine)
+    unrolled(parts, last_theirs)
 
     for part in range(parts):
         swap_of(fl_own, fl_got, part, part).wait_send()

time: 62.4 us -> 61.6 us (0.987)
  Pallas kernels: 61.6 us -> 60.8 us
    pallas_call x1, Pallas kernels: 60.5 us -> 59.8 us  [body(): pl.pallas_call(functools.partial(kernel, chips, ranks, float(wide * ranks...]
where the time goes in v8:
time: 61.6 us; the launch traced here: 61.5 us
  Pallas kernels  60.8 us (99%)
  between operations  0.64 us (1%)
    pallas_call x1, Pallas kernels, body(): pl.pallas_call(functools.partial(kernel, chips, ranks, float(wide * ranks...  59.8 us

profile of v8, /device:TPU:1, one launch (start us, length us, event | category | flops | bytes accessed | tf_op | source)
XLA Modules:
  0.0 61.5 jit_solution(9613459194897520265)
XLA Ops:
  0.6 59.8 %layer.1 = (f32[256,1024]{1,0:T(8,128)S(1)}, f32[256,128]{1,0:T(8,128)S(1)}, f32[256,128]{1,0:T(8,128)S(1)}, f32[4,8,256]{2,1,0:T(8,128)S(1)}, f32[256,128]{1,0:T(8,128)S(1)}, /*index=5*/f32[8,128]{1,0:T(8,128)S(1)}) custom-call(bf16[256,1024]{1,0:T(8,128)(2,1)} %x_hbm.1, bf16[256,1024]{1,0:T(8,128)(2,1)} %target_hbm.1, bf16[256,128]{1,0:T(8,128)(2,1)} %bitcast.11, ...), custom_call_target="tpu_custom_call" | custom-call | tf_op jit(solution)/shard_map/layer/pallas_call | solution.py:613
  60.4 1.1 %finish.1 = (f32[256,1024]{1,0:T(8,128)}, f32[256,128]{1,0:T(8,128)}, f32[256,128]{1,0:T(8,128)}, f32[8,256]{1,0:T(8,128)}) custom-call(f32[256,1024]{1,0:T(8,128)S(1)} %get-tuple-element.14.gx_in, f32[256,128]{1,0:T(8,128)S(1)} %get-tuple-element.15.gb_in, f32[256,128]{1,0:T(8,128)S(1)} %get-tuple-element.16.gc_in, ...), custom_call_target="tpu_custom_call" | custom-call | tf_op jit(solution)/shard_map/finish/pallas_call | solution.py:672

commit v9 on v8

--- a/solution.py
+++ b/solution.py
@@ -557,7 +557,9 @@
 
 
 def finish(gx_in, gb_in, gc_in, rows_ref, rq_ref, ext_ref, gx_ref, gb_ref, gc_ref, gs_ref, sums_ref, sems):
-    pairs = ((gx_in, gx_ref), (gb_in, gb_ref), (gc_in, gc_ref))
+    rows = gx_in.shape[0] // 8
+    blocks = [pl.ds(i * rows, rows) for i in range(8)]
+    pairs = [(gx_in.at[block], gx_ref.at[block]) for block in blocks] + [(gb_in, gb_ref), (gc_in, gc_ref)]
     copies = [pltpu.make_async_copy(source, target, sems.at[i]) for i, (source, target) in enumerate(pairs)]
     for copy in copies:
         copy.start()
@@ -572,7 +574,7 @@
     high, mid, low = split3(ends[0:heads, :] - step * inner_x)
     grad_dec = mm(high, lower) + (mm(mid, lower) + mm(low, lower)) + extra
     sums_ref[...] = inner_x - rate * grad_dec
-    last = pltpu.make_async_copy(sums_ref, gs_ref, sems.at[3])
+    last = pltpu.make_async_copy(sums_ref, gs_ref, sems.at[10])
     last.start()
     for copy in copies:
         copy.wait()
@@ -674,7 +676,7 @@
         out_shape=out_shape,
         in_specs=[pl.BlockSpec(memory_space=pl.ANY)] * 3 + [vmem] * 3,
         out_specs=[hbm] * 4,
-        scratch_shapes=[buffer(heads, tokens), pltpu.SemaphoreType.DMA((4,))],
+        scratch_shapes=[buffer(heads, tokens), pltpu.SemaphoreType.DMA((11,))],
         compiler_params=pltpu.CompilerParams(vmem_limit_bytes=4 * 1024 * 1024),
         name="finish",
     )(*results)

time: 61.6 us -> 61.7 us (level)
  no operation moved by 1% of the time
where the time goes in v9:
time: 61.7 us; the launch traced here: 61.6 us
  Pallas kernels  60.9 us (99%)
  between operations  0.64 us (1%)
    pallas_call x1, Pallas kernels, body(): pl.pallas_call(functools.partial(kernel, chips, ranks, float(wide * ranks...  59.8 us

profile of v9, /device:TPU:1, one launch (start us, length us, event | category | flops | bytes accessed | tf_op | source)
XLA Modules:
  0.0 61.6 jit_solution(14078756726658230389)
XLA Ops:
  0.6 59.8 %layer.1 = (f32[256,1024]{1,0:T(8,128)S(1)}, f32[256,128]{1,0:T(8,128)S(1)}, f32[256,128]{1,0:T(8,128)S(1)}, f32[4,8,256]{2,1,0:T(8,128)S(1)}, f32[256,128]{1,0:T(8,128)S(1)}, /*index=5*/f32[8,128]{1,0:T(8,128)S(1)}) custom-call(bf16[256,1024]{1,0:T(8,128)(2,1)} %x_hbm.1, bf16[256,1024]{1,0:T(8,128)(2,1)} %target_hbm.1, bf16[256,128]{1,0:T(8,128)(2,1)} %bitcast.11, ...), custom_call_target="tpu_custom_call" | custom-call | tf_op jit(solution)/shard_map/layer/pallas_call | solution.py:615
  60.4 1.1 %finish.1 = (f32[256,1024]{1,0:T(8,128)}, f32[256,128]{1,0:T(8,128)}, f32[256,128]{1,0:T(8,128)}, f32[8,256]{1,0:T(8,128)}) custom-call(f32[256,1024]{1,0:T(8,128)S(1)} %get-tuple-element.14.gx_in, f32[256,128]{1,0:T(8,128)S(1)} %get-tuple-element.15.gb_in, f32[256,128]{1,0:T(8,128)S(1)} %get-tuple-element.16.gc_in, ...), custom_call_target="tpu_custom_call" | custom-call | tf_op jit(solution)/shard_map/finish/pallas_call | solution.py:674
